TPU v7x, 512 devices: a whole 4x8x8 slice. The times are simulated.
512 devices in a mesh: dp: 4 (over x), ctx: 16 (over z_hi, y), head: 8 (over z_lo, core).
Axes of the slice: x: 4, y: 8, z: 8 (z_hi: 2, z_lo: 4; z = z_hi * 4 + z_lo), core: 2. Of those that a mesh axis runs over, the one named last changes fastest.
Arguments:
- queries: bfloat16 [4, 2560, 8192], P('dp', 'ctx', 'head'), may hold values from -6 to 6
- keys_values: bfloat16 [2, 4, 2560, 1024], P(None, 'dp', 'ctx', 'head'), may hold values from -6 to 6
- out_grad: bfloat16 [4, 2560, 8192], P('dp', 'ctx', 'head'), may hold values from -6 to 6
- activations: bfloat16 [4, 2560, 8192], P('dp', 'ctx', 'head'), may hold values from -6 to 6
- adapter_down: bfloat16 [3, 16, 8192], P(None, None, 'head'), may hold values from -0.0625 to 0.0625
- adapter_up_q: bfloat16 [16, 8192], P(None, 'head'), may hold values from -0.0625 to 0.0625
- adapter_up_kv: bfloat16 [2, 16, 1024], P(None, None, 'head'), may hold values from -0.1875 to 0.1875
- doc_lengths: int32 [4, 8], P('dp'), may hold values from 1 to 1280, 2560 in all within a row
- block_order: int32 [32], replicated, may hold values from 0 to 31, each once
Outputs:
- grad_queries: bfloat16 [4, 2560, 8192], P('dp', 'ctx', 'head')
- grad_keys_values: bfloat16 [2, 4, 2560, 1024], P(None, 'dp', 'ctx', 'head')
- grad_down: float32 [3, 16, 8192], P(None, None, 'head')
- grad_up_q: float32 [16, 8192], P(None, 'head')
- grad_up_kv: float32 [2, 16, 1024], P(None, None, 'head')
Inputs may be any that keep to these rules, and one draw needn't show every extreme that they name: `doc_lengths`: each row sums to 2560; its largest entry is exactly 1280. `block_order`: each of 0 .. 31 once.
All inputs are finite; a program needn't handle non-finite values.
Results may differ from a plain program's by a relative error of at most 0.017.
Values may be sent and summed in bfloat16 or wider, within the bound.
A program may use at most 64 MiB of HBM per device.

v0:
```python
import math

import jax
import jax.numpy as jnp
from jax import lax
from jax.sharding import PartitionSpec as P

neg_large = -1e30
adapter_scale = 2.0


def visible_pairs(query_pos, query_doc, key_pos, key_doc):
    return (key_pos[None, :] <= query_pos[:, None]) & (key_doc[None, :] == query_doc[:, None])


def on_device(
    queries,
    keys_values,
    out_grad,
    activations,
    adapter_down,
    adapter_up_q,
    adapter_up_kv,
    doc_lengths,
    block_order,
):
    row_count = queries.shape[1]
    block_rows = row_count // 2
    head_dim = keys_values.shape[3]
    group_size = queries.shape[2] // head_dim
    context_size = lax.axis_size("ctx")
    seq_rows = row_count * context_size
    slot_count = block_order.shape[0]
    my_index = lax.axis_index("ctx")
    factor = 1.0 / math.sqrt(head_dim)
    row_index = jnp.arange(seq_rows, dtype=jnp.int32)
    slot_match = (row_index // block_rows)[:, None] == jnp.arange(slot_count, dtype=jnp.int32)[
        None, :
    ]
    positions = (
        jnp.sum(jnp.where(slot_match, block_order[None, :], 0), axis=1) * block_rows
        + row_index % block_rows
    )
    bounds = jnp.cumsum(doc_lengths[0])
    documents = jnp.sum((positions[:, None] >= bounds[None, :]).astype(jnp.int32), axis=1)
    query_pos = lax.dynamic_slice_in_dim(positions, my_index * row_count, row_count)
    query_doc = lax.dynamic_slice_in_dim(documents, my_index * row_count, row_count)
    query_tile = queries[0].reshape(row_count, group_size, head_dim)
    grad_out = out_grad[0].reshape(row_count, group_size, head_dim)
    partial_low = jnp.einsum(
        "ld,jrd->jlr", activations[0], adapter_down, preferred_element_type=jnp.float32
    )
    low_inputs = lax.psum(partial_low, "head").astype(jnp.bfloat16)
    gathered = lax.all_gather(keys_values, "ctx", axis=2, tiled=True)
    key_all = gathered[0, 0]
    value_all = gathered[1, 0]
    visible_all = visible_pairs(query_pos, query_doc, positions, documents)

    def head_step(collected, items):
        query_head, grad_head = items
        scores = (
            jnp.einsum("rd,nd->rn", query_head, key_all, preferred_element_type=jnp.float32)
            * factor
        )
        scores = jnp.where(visible_all, scores, neg_large)
        largest = jnp.max(scores, axis=1, keepdims=True)
        weights = jnp.where(visible_all, jnp.exp(scores - largest), 0.0)
        probs = weights / jnp.sum(weights, axis=1, keepdims=True)
        slopes = jnp.einsum("rd,nd->rn", grad_head, value_all, preferred_element_type=jnp.float32)
        mean_head = jnp.sum(probs * slopes, axis=1, keepdims=True)
        score_grads = (probs * (slopes - mean_head) * factor).astype(jnp.bfloat16)
        probs_low = probs.astype(jnp.bfloat16)
        query_grad = jnp.dot(score_grads, key_all, preferred_element_type=jnp.float32)
        grad_key = jnp.einsum(
            "rn,rd->nd", score_grads, query_head, preferred_element_type=jnp.float32
        )
        grad_value = jnp.einsum(
            "rn,rd->nd", probs_low, grad_head, preferred_element_type=jnp.float32
        )
        return (collected + jnp.stack([grad_key, grad_value]), query_grad)

    key_terms, head_queries = lax.scan(
        head_step,
        jnp.zeros((2, seq_rows, head_dim), jnp.float32),
        (jnp.moveaxis(query_tile, 1, 0), jnp.moveaxis(grad_out, 1, 0)),
    )
    grad_query = jnp.moveaxis(head_queries, 0, 1)
    grad_pair = lax.psum_scatter(
        key_terms.astype(jnp.bfloat16), "ctx", scatter_dimension=1, tiled=True
    )
    grad_q_low = grad_query.astype(jnp.bfloat16).reshape(row_count, group_size * head_dim)
    low_grad_parts = jnp.concatenate(
        [
            jnp.einsum("lc,rc->lr", grad_q_low, adapter_up_q, preferred_element_type=jnp.float32)[
                None
            ],
            jnp.einsum(
                "jlc,jrc->jlr", grad_pair, adapter_up_kv, preferred_element_type=jnp.float32
            ),
        ],
        axis=0,
    )
    low_grads = lax.psum(low_grad_parts, "head").astype(jnp.bfloat16)
    down_terms = jnp.einsum(
        "jlr,ld->jrd", low_grads, activations[0], preferred_element_type=jnp.float32
    )
    up_q_terms = jnp.einsum(
        "lr,lc->rc", low_inputs[0], grad_q_low, preferred_element_type=jnp.float32
    )
    up_kv_terms = jnp.einsum(
        "jlr,jlc->jrc", low_inputs[1:], grad_pair, preferred_element_type=jnp.float32
    )
    summed = lax.psum((down_terms, up_q_terms, up_kv_terms), ("dp", "ctx"))
    norm = adapter_scale / math.sqrt(lax.axis_size("dp") * seq_rows)
    return (
        grad_q_low.reshape(1, row_count, group_size * head_dim),
        grad_pair.reshape(2, 1, row_count, head_dim),
        summed[0] * norm,
        summed[1] * norm,
        summed[2] * norm,
    )


def solution(mesh):
    placed = (
        P("dp", "ctx", "head"),
        P(None, "dp", "ctx", "head"),
        P("dp", "ctx", "head"),
        P("dp", "ctx", "head"),
        P(None, None, "head"),
        P(None, "head"),
        P(None, None, "head"),
        P("dp", None),
        P(),
    )
    return jax.shard_map(
        on_device,
        mesh=mesh,
        in_specs=placed,
        out_specs=(
            P("dp", "ctx", "head"),
            P(None, "dp", "ctx", "head"),
            P(None, None, "head"),
            P(None, "head"),
            P(None, None, "head"),
        ),
        check_vma=False,
    )
```

profile of v0, /device:TPU:64, one launch (start us, length us, event | category | flops | bytes accessed | tf_op | source)
XLA Modules:
  0.0 1222.1 jit_solution(15978050023125801163)
XLA Ops:
  7.2 0.7 all-gather.2.cloned.1.call-update
  8.0 0.8 reduce-window.8
  8.8 0.8 select_reduce_fusion
  9.9 1.0 copy.24
  10.9 0.8 copy.19
  11.7 1.0 copy.25
  12.8 0.8 copy.20
  13.5 95.6 %all-gather.2.cloned.1.call-done = bf16[2,1,2560,128]{3,2,1,0:T(8,128)(2,1)} async-done(((bf16[2,1,160,128]{3,2,1,0:T(8,128)(2,1)}), bf16[2,1,2560,128]{3,2,1,0:T(8,128)(2,1)}) %all-gather.2.cloned.1.call-update) | async-done | bytes 1310736 | tf_op jit(solution)/shard_map/all_gather | solution.py:54
  109.1 2.5 slice_bitcast_fusion
  111.5 65.5 %while.13 = (s32[]{:T(128)}, f32[2,2560,128]{2,1,0:T(8,128)S(1)}, bf16[8,160,128]{2,1,0:T(8,128)(2,1)S(1)}, bf16[8,160,128]{2,1,0:T(8,128)(2,1)}, bf16[2560,128]...) while((s32[]{:T(128)}, f32[2,2560,128]{2,1,0:T(8,128)S(1)}, ...), condition=%wide.region_7.8_spmd.clone, body=%wide.region_3.7_spmd.clone.sunk | while | flops 536493600 | bytes 33575256 | solution.py:82
  111.6 1.8 fusion.74
  113.4 0.6 fusion.75
  114.0 1.6 multiply_reduce_fusion.2
  115.8 1.4 convolution_bitcast_fusion.7
  117.6 1.3 convolution_bitcast_fusion.8
  119.0 0.7 maximum_add_fusion.2
  119.7 1.8 fusion.74
  122.1 1.6 multiply_reduce_fusion.2
  124.0 1.4 convolution_bitcast_fusion.7
  125.8 1.3 convolution_bitcast_fusion.8
  127.2 0.7 maximum_add_fusion.2
  127.9 1.8 fusion.74
  130.3 1.6 multiply_reduce_fusion.2
  132.2 1.4 convolution_bitcast_fusion.7
  134.0 1.3 convolution_bitcast_fusion.8
  135.4 0.7 maximum_add_fusion.2
  136.1 1.8 fusion.74
  138.5 1.6 multiply_reduce_fusion.2
  140.4 1.4 convolution_bitcast_fusion.7
  142.2 1.3 convolution_bitcast_fusion.8
  143.6 0.7 maximum_add_fusion.2
  144.3 1.8 fusion.74
  146.7 1.6 multiply_reduce_fusion.2
  148.6 1.4 convolution_bitcast_fusion.7
  150.4 1.3 convolution_bitcast_fusion.8
  151.8 0.7 maximum_add_fusion.2
  152.5 1.8 fusion.74
  154.9 1.6 multiply_reduce_fusion.2
  156.8 1.4 convolution_bitcast_fusion.7
  158.6 1.3 convolution_bitcast_fusion.8
  159.9 0.7 maximum_add_fusion.2
  160.7 1.8 fusion.74
  163.1 1.6 multiply_reduce_fusion.2
  165.0 1.4 convolution_bitcast_fusion.7
  166.8 1.3 convolution_bitcast_fusion.8
  168.1 0.7 maximum_add_fusion.2
  168.9 1.8 fusion.74
  171.3 1.6 multiply_reduce_fusion.2
  173.2 1.4 convolution_bitcast_fusion.7
  175.0 1.3 convolution_bitcast_fusion.8
  176.3 0.7 maximum_add_fusion.2
  177.1 1.2 convert_element_type.27
  178.8 0.9 reshape_reshape.3
  179.8 220.8 %reduce-scatter.2.cloned.1.call-done = bf16[2,160,128]{2,1,0:T(8,128)(2,1)} async-done(((bf16[2,2560,128]{2,1,0:T(8,128)(2,1)}), bf16[2,160,128]{2,1,0:T(8,128)(2,1)}) %reduce-scatter.2.cloned.1.call-update) | async-done | bytes 81936 | tf_op jit(solution)/shard_map/reduce_scatter | solution.py:88
  400.7 1.0 fusion.39
  401.7 24.7 %all-reduce.1 = (bf16[3,160,16]{1,2,0:T(8,128)(2,1)S(1)}, bf16[3,160,16]{1,2,0:T(8,128)(2,1)S(1)}) all-reduce(f32[3,160,16]{1,2,0:T(8,128)S(1)} %pad_maximum_fusion, f32[3,160,16]{1,2,0:T(8,128)S(1)} %convolution_bitcast_fusion.3), channel_id=1, replica_groups=mesh['dp'=4,'ctx'=16,'head'=8] {'head'}, use_global_device_ids=true, to_apply=%region_9.10 | all-reduce | flops 15360 | bytes 92160 | tf_op jit(solution)/shard_map/psum | solution.py:103
  426.5 0.8 fusion.20
  427.3 0.9 fusion.24
  428.2 1.0 fusion.40
  429.2 431.7 %psum.39 = f32[2,16,128]{2,1,0:T(8,128)S(1)} all-reduce(f32[2,16,128]{2,1,0:T(8,128)S(1)} %fusion.40), channel_id=1, replica_groups=mesh['dp'=4,'ctx'=16,'head'=8] {'dp','ctx'}, use_global_device_ids=true, to_apply=%region_13.14 | all-reduce | flops 4096 | bytes 32768 | tf_op jit(solution)/shard_map/psum | solution.py:113
  860.8 0.6 broadcast_multiply_fusion.2
  861.4 351.1 %all-reduce.4.cloned.1.call-done = (f32[3,16,1024]{2,1,0:T(8,128)}, f32[16,1024]{1,0:T(8,128)}) async-done(((f32[3,16,1024]{2,1,0:T(8,128)}, f32[16,1024]{1,0:T(8,128)}), (f32[3,16,1024]{2,1,0:T(8,128)}, f32[16,1024]{1,0:T(8,128)})) %all-reduce.4.cloned.1.call-update) | async-done | bytes 262160 | tf_op jit(solution)/shard_map/psum | solution.py:113
  1212.5 1.6 broadcast_multiply_fusion
  1214.1 1.5 broadcast_multiply_fusion.1
  (79 shorter events, 10.4 us)
Async XLA Ops:
  7.2 171.2 %copy-start = (bf16[1,160,1024]{2,1,0:T(8,128)(2,1)S(1)}, bf16[1,160,1024]{2,1,0:T(8,128)(2,1)}, u32[]{:S(2)}) copy-start(bf16[1,160,1024]{2,1,0:T(8,128)(2,1)} %param.14) | copy-start | bytes 983044
  7.2 101.9 %all-gather.2.cloned.1.call-start = ((), (), s32[]{:S(2)}) async-start(), calls=%async_computation.1 | async-start | bytes 1392640 | tf_op jit(solution)/shard_map/all_gather | solution.py:54
  7.9 392.8 %reduce-scatter.2.cloned.1.call-start = ((), (), s32[]{:S(2)}) async-start(), calls=%async_computation.2 | async-start | bytes 1392640 | tf_op jit(solution)/shard_map/reduce_scatter | solution.py:88
  111.5 2.4 copy-start.2
  115.8 1.4 copy-start.1
  119.7 2.4 copy-start.2
  124.0 1.4 copy-start.1
  127.9 2.4 copy-start.2
  132.2 1.4 copy-start.1
  136.1 2.4 copy-start.2
  140.4 1.4 copy-start.1
  144.3 2.4 copy-start.2
  148.6 1.4 copy-start.1
  152.5 2.4 copy-start.2
  156.8 1.4 copy-start.1
  160.7 2.4 copy-start.2
  165.0 1.4 copy-start.1
  168.9 2.4 copy-start.2
  173.2 1.4 copy-start.1
  177.1 1.3 copy-start.3
  178.3 1.3 copy-start.5
  178.3 222.4 %copy-start.4 = (bf16[2,16,128]{2,1,0:T(8,128)(2,1)S(1)}, bf16[2,16,128]{2,1,0:T(8,128)(2,1)}, u32[]{:S(2)}) copy-start(bf16[2,16,128]{2,1,0:T(8,128)(2,1)} %param.17) | copy-start | bytes 24580
  178.4 1034.2 %all-reduce.4.cloned.1.call-start = ((), (), s32[]{:S(2)}) async-start(), calls=%async_computation.3 | async-start | bytes 524288 | tf_op jit(solution)/shard_map/psum | solution.py:113
Sparse Core Ops, SparseCore 0:
  11.1 97.9 all-gather.1
  178.5 222.1 reduce-scatter.1
  428.3 784.1 all-reduce.3
where the time goes:
time: 1220 us
  waiting for transfers between devices  668 us (55%)
  blocking collectives  456 us (37%)
  matrix products  56.3 us (5%)
  other arithmetic  19.4 us (2%)
  between operations  13.9 us (1%)
    psum x1, blocking collectives, on_device(): summed = lax.psum((down_terms, up_q_terms, up_kv_terms), ('dp', 'ctx'))  432 us
    psum x1, waiting for transfers between devices, on_device(): summed = lax.psum((down_terms, up_q_terms, up_kv_terms), ('dp', 'ctx'))  351 us
    reduce_scatter x1, waiting for transfers between devices, on_device(): lax.psum_scatter(key_terms.astype(jnp.bfloat16), 'ctx', scatter_dimension...  221 us
    all_gather x1, waiting for transfers between devices, on_device(): gathered = lax.all_gather(keys_values, 'ctx', axis=2, tiled=True)  95.6 us
    psum x1, blocking collectives, on_device(): low_grads = lax.psum(low_grad_parts, 'head').astype(jnp.bfloat16)  24.7 us
  transfers between devices with their start and end apart: 3, of which 3 were waited for; matrix products, arithmetic and copies ran while one was open for 1% of the time, Pallas kernels for 0%

commit v1 on v0

v1 whole, which is shorter than its diff:
```python
import functools
import math

import jax
import jax.numpy as jnp
from jax import lax
from jax.experimental import pallas as pl
from jax.experimental.pallas import tpu as pltpu
from jax.sharding import PartitionSpec as P

MESH = pl.DeviceIdType.MESH
BF16 = jnp.bfloat16
F32 = jnp.float32
VMEM = pltpu.VMEM
NT = (((1,), (1,)), ((), ()))
NN = (((1,), (0,)), ((), ()))
TN = (((0,), (0,)), ((), ()))
ADAPTER_SCALE = 2.0
NEG_LARGE = -1e30
TILE = 272


def dot(a, b, dims):
    return lax.dot_general(a, b, dims, preferred_element_type=F32)


def remote(src, dst, send_sem, recv_sem, device):
    return pltpu.make_async_remote_copy(
        src_ref=src,
        dst_ref=dst,
        send_sem=send_sem,
        recv_sem=recv_sem,
        device_id=device,
        device_id_type=MESH,
    )


def greet(devices):
    barrier = pltpu.get_barrier_semaphore()
    for device in devices:
        pl.semaphore_signal(barrier, inc=1, device_id=device, device_id_type=MESH)
    return barrier


def ring_order(steps):
    order = [(0, 0)]
    for s in range(1, steps):
        order += [(0, s), (1, s - 1)]
    return order + [(1, steps - 1)]


def gather_kernel(ys, kv_ref, out_ref, z_sems, send_sems, recv_sems):
    c = lax.axis_index("ctx")
    y, z = c % ys, c // ys
    far = ys // 2
    partner = (1 - z) * ys + y
    right = z * ys + (y + 1) % ys
    left = z * ys + (y + ys - 1) % ys
    barrier = greet([{"ctx": right}, {"ctx": left}, {"ctx": partner}])
    pl.semaphore_wait(barrier, 3)

    across = remote(
        kv_ref, out_ref.at[:, c], z_sems.at[0], z_sems.at[1], {"ctx": partner}
    )
    across.start()

    def hop(u, d, s, origin):
        slot = (z if u == 0 else 1 - z) * ys + origin % ys
        whole = out_ref.at[:, slot]
        dst = out_ref.at[d, slot] if s == far - 1 else whole
        src = kv_ref if (s == 0 and u == 0) else whole
        if s == far - 1:
            src = out_ref.at[d, slot]
        return remote(
            src, dst, send_sems.at[u, d, s], recv_sems.at[u, d, s],
            {"ctx": right if d == 0 else left},
        )

    def sent(u, d, s):
        return hop(u, d, s, y + ys - s if d == 0 else y + s)

    def landed(u, d, s):
        return hop(u, d, s, y + ys - 1 - s if d == 0 else y + 1 + s)

    for u, s in ring_order(far):
        if u == 1 and s == 0:
            across.wait_recv()
        for d in range(2):
            if s > 0:
                landed(u, d, s - 1).wait_recv()
            sent(u, d, s).start()
        if u == 0 and s == 0:
            out_ref[:, c] = kv_ref[...]
    for u in range(2):
        for d in range(2):
            landed(u, d, far - 1).wait_recv()
    across.wait_send()
    for u in range(2):
        for d in range(2):
            for s in range(far):
                sent(u, d, s).wait_send()


def attention_kernel(
    group, block, slots, docs,
    order_ref, lengths_ref, q_ref, g_ref, kv_ref, gq_ref, parts_ref,
    inverse, ks, vs, s_scr, p_scr, acc,
):
    pad = TILE
    head = q_ref.shape[1] // group
    lanes = group * block
    factor = 1.0 / math.sqrt(head)
    mine = lax.axis_index("ctx") * 2

    def invert(i, _):
        inverse[order_ref[i]] = i
        return 0

    lax.fori_loop(0, slots, invert, 0)
    ks[:pad] = jnp.zeros((pad, head), BF16)
    vs[:pad] = jnp.zeros((pad, head), BF16)

    def sort(p, _):
        slot = inverse[p]
        dst = pl.ds(pl.multiple_of(pad + p * block, 16), block)
        src = pl.ds(pl.multiple_of(slot * block, 16), block)
        ks[dst, :] = kv_ref[0, src, :]
        vs[dst, :] = kv_ref[1, src, :]
        return 0

    lax.fori_loop(0, slots, sort, 0)
    acc[...] = jnp.zeros(acc.shape, F32)

    lane = lax.broadcasted_iota(jnp.int32, (1, lanes), 1)
    row = lane
    for g in range(1, group):
        row = jnp.where(lane >= g * block, lane - g * block, row)
    sub = lax.broadcasted_iota(jnp.int32, (TILE, lanes), 0)

    for half in range(2):
        place = order_ref[mine + half]
        first = place * block
        pos = row + first
        begin = jnp.zeros((1, lanes), jnp.int32)
        begin_first = 0
        bound = 0
        for i in range(docs):
            bound = bound + lengths_ref[0, i]
            begin = jnp.where(pos >= bound, bound, begin)
            begin_first = jnp.where(first >= bound, bound, begin_first)
        end = first + block
        tiles = (end - begin_first + TILE - 1) // TILE
        rows = slice(half * block, (half + 1) * block)
        q = jnp.concatenate(
            [q_ref[rows, g * head : (g + 1) * head] for g in range(group)], axis=0
        )
        go = jnp.concatenate(
            [g_ref[rows, g * head : (g + 1) * head] for g in range(group)], axis=0
        )

        def keys_at(t):
            return pl.ds(pl.multiple_of(pad + end - (t + 1) * TILE, 16), TILE)

        def hold_at(t):
            return pl.ds(pl.multiple_of(t * TILE, 16), TILE)

        def score(t, most):
            at = end - (t + 1) * TILE
            s = dot(ks[keys_at(t), :], q, NT) * (factor * math.log2(math.e))
            seen = (sub >= begin - at) & (sub <= pos - at)
            s = jnp.where(seen, s, NEG_LARGE)
            s_scr[hold_at(t), :] = s
            return jnp.maximum(most, jnp.max(s.reshape(TILE // 8, 8, lanes), axis=0))

        most = lax.fori_loop(0, tiles, score, jnp.full((8, lanes), NEG_LARGE, F32))
        most = jnp.max(most, axis=0, keepdims=True)

        def weigh(t, sums):
            total, slope = sums
            w = jnp.exp2(s_scr[hold_at(t), :] - most)
            s_scr[hold_at(t), :] = w
            d = dot(vs[keys_at(t), :], go, NT)
            p_scr[hold_at(t), :] = d
            total = total + jnp.sum(w.reshape(TILE // 8, 8, lanes), axis=0)
            slope = slope + jnp.sum((w * d).reshape(TILE // 8, 8, lanes), axis=0)
            return total, slope

        zero = jnp.zeros((8, lanes), F32)
        total, slope = lax.fori_loop(0, tiles, weigh, (zero, zero))
        over = 1.0 / jnp.sum(total, axis=0, keepdims=True)
        mean = jnp.sum(slope, axis=0, keepdims=True) * over

        def grads(t, gq):
            prob = s_scr[hold_at(t), :] * over
            ds = (prob * (p_scr[hold_at(t), :] - mean)).astype(BF16)
            acc[1, keys_at(t), :] += dot(prob.astype(BF16), go, NN)
            acc[0, keys_at(t), :] += dot(ds, q, NN)
            return gq + dot(ks[keys_at(t), :], ds, TN)

        gq = lax.fori_loop(0, tiles, grads, jnp.zeros((head, lanes), F32))
        gq = (gq * factor).T.astype(BF16)
        for g in range(group):
            gq_ref[rows, g * head : (g + 1) * head] = gq[g * block : (g + 1) * block]

    def unsort(p, _):
        slot = inverse[p]
        src = pl.ds(pl.multiple_of(pad + p * block, 16), block)
        dst = pl.ds(pl.multiple_of(slot * block, 16), block)
        parts_ref[0, dst, :] = (acc[0, src, :] * factor).astype(BF16)
        parts_ref[1, dst, :] = acc[1, src, :].astype(BF16)
        return 0

    lax.fori_loop(0, slots, unsort, 0)


def reduce_kernel(
    ys, xs, heads, norm,
    parts_ref, gq_ref, act_ref, down_ref, upq_ref, upkv_ref,
    gkv_ref, gdown_ref, gupq_ref, gupkv_ref,
    slots, cross, low_a, low_b, y_out, y_in, g_in, a_in,
    ring_send, ring_recv, cross_sem, la_send, la_recv, lb_send, lb_recv,
    y_send, y_recv, g_send, g_recv, a_send, a_recv,
):
    dp, c, h = lax.axis_index("dp"), lax.axis_index("ctx"), lax.axis_index("head")
    y, z = c % ys, c // ys
    far = ys // 2
    rank = upq_ref.shape[0]
    group = 2 * xs
    partner = {"ctx": (1 - z) * ys + y}
    right = {"ctx": z * ys + (y + 1) % ys}
    left = {"ctx": z * ys + (y + ys - 1) % ys}
    y_peers = [{"ctx": z * ys + (y + k) % ys} for k in range(1, ys)]
    h_peers = [{"head": (h + k) % heads} for k in range(1, heads)]
    me_g = dp * 2 + z
    g_peers = []
    for k in range(1, group):
        other = (me_g + k) % group
        g_peers.append({"dp": other // 2, "ctx": (other % 2) * ys + y})

    barrier = greet(y_peers + h_peers + g_peers)

    act = act_ref[...]
    gq = gq_ref[...]
    low_a[h, : 3 * rank, :] = dot(down_ref[...], act, NT).astype(BF16)
    low_a[h, 3 * rank :, :] = dot(upq_ref[...], gq, NT).astype(BF16)
    pl.semaphore_wait(barrier, ys - 1 + heads - 1 + group - 1)

    def steps_of(j, d):
        return far if j == d else far - 1

    def target(j, d, s):
        away = steps_of(j, d) - s
        return (y + away) % ys if d == 0 else (y + ys - away) % ys

    def part(j, u, at):
        return parts_ref.at[j, ((1 - z) if u == 0 else z) * ys + at]

    def hop(j, d, u, s):
        src = part(j, u, target(j, d, 0)) if s == 0 else slots.at[j, d, u, s - 1]
        return remote(
            src, slots.at[j, d, u, s], ring_send.at[j, d, u, s],
            ring_recv.at[j, d, u, s], right if d == 0 else left,
        )

    def advance(u, s):
        for j in range(2):
            for d in range(2):
                if s >= steps_of(j, d):
                    continue
                if s > 0:
                    hop(j, d, u, s - 1).wait_recv()
                    here = slots[j, d, u, s - 1].astype(F32)
                    more = part(j, u, target(j, d, s))[...].astype(F32)
                    slots[j, d, u, s - 1] = (here + more).astype(BF16)
                hop(j, d, u, s).start()

    def finish(j, u):
        total = part(j, u, y)[...].astype(F32)
        for d in range(2):
            hop(j, d, u, steps_of(j, d) - 1).wait_recv()
            total = total + slots[j, d, u, steps_of(j, d) - 1].astype(F32)
        return total

    def cross_hop(j):
        return remote(
            cross.at[0, j], cross.at[1, j], cross_sem.at[0, j], cross_sem.at[1, j], partner
        )

    def spread(buffer, me, peers, size, send, recv):
        def one(k, slot):
            return remote(
                buffer.at[slot], buffer.at[slot], send.at[k], recv.at[k], peers[k]
            )

        def start():
            for k in range(size - 1):
                one(k, me).start()

        def arrive():
            for k in range(size - 1):
                one(k, (me + size - 1 - k) % size).wait_recv()

        def drain():
            for k in range(size - 1):
                one(k, me).wait_send()

        return start, arrive, drain

    def total_of(buffer, size):
        total = buffer[0].astype(F32)
        for k in range(1, size):
            total = total + buffer[k].astype(F32)
        return total

    la_start, la_arrive, la_drain = spread(low_a, h, h_peers, heads, la_send, la_recv)
    lb_start, lb_arrive, lb_drain = spread(low_b, h, h_peers, heads, lb_send, lb_recv)
    g_start, g_arrive, g_drain = spread(g_in, me_g, g_peers, group, g_send, g_recv)
    a_start, a_arrive, a_drain = spread(a_in, y, y_peers, ys, a_send, a_recv)

    order = ring_order(far)
    advance(*order[0])
    la_start()
    width = act.shape[1] // ys

    for i, (u, s) in enumerate(order[1:]):
        advance(u, s)
        if i == 2:
            la_arrive()
            low = total_of(low_a, heads).astype(BF16)
            first = dot(low[3 * rank :], act, NN).astype(BF16)
            second = dot(low[:rank], gq, NN).astype(BF16)
            for k in range(ys):
                y_out[k, :rank, :] = first[:, k * width : (k + 1) * width]
                y_out[k, rank : 2 * rank, :] = second[:, k * width : (k + 1) * width]
        if (u, s) == (0, far - 1):
            pass
    for j in range(2):
        cross[0, j] = finish(j, 0).astype(BF16)
        cross_hop(j).start()
    for j in range(2):
        total = finish(j, 1)
        cross_hop(j).wait_recv()
        gkv = (total + cross[1, j].astype(F32)).astype(BF16)
        gkv_ref[j] = gkv
        low_b[h, j * rank : (j + 1) * rank, :] = dot(upkv_ref[j], gkv, NT).astype(BF16)
    lb_start()
    for k in range(2, ys):
        y_out[k, 4 * rank :, :] = jnp.zeros((rank, width), BF16)
    for j in range(2):
        y_out[j, 4 * rank :, :] = dot(
            low[(1 + j) * rank : (2 + j) * rank], gkv_ref[j], NN
        ).astype(BF16)
    lb_arrive()
    low_kv = total_of(low_b, heads).astype(BF16)
    both = dot(low_kv, act, NN).astype(BF16)
    for k in range(ys):
        y_out[k, 2 * rank : 4 * rank, :] = both[:, k * width : (k + 1) * width]

    def y_hop(k, to, slot):
        return remote(y_out.at[to], y_in.at[slot], y_send.at[k], y_recv.at[k], y_peers[k])

    for k in range(ys - 1):
        y_hop(k, (y + 1 + k) % ys, y).start()
    y_in[y] = y_out[y]
    for k in range(ys - 1):
        y_hop(k, 0, (y + ys - 1 - k) % ys).wait_recv()
    g_in[me_g] = total_of(y_in, ys).astype(BF16)
    g_start()
    g_arrive()
    a_in[y] = (total_of(g_in, group) * norm).astype(BF16)
    a_start()
    a_arrive()
    for k in range(ys):
        piece = a_in[k].astype(F32)
        at = slice(k * width, (k + 1) * width)
        gdown_ref[:rank, at] = piece[:rank]
        gupq_ref[:, at] = piece[rank : 2 * rank]
        gdown_ref[rank:, at] = piece[2 * rank : 4 * rank]
        if k < 2:
            gupkv_ref[k] = piece[4 * rank :]

    la_drain()
    lb_drain()
    g_drain()
    a_drain()
    for k in range(ys - 1):
        y_hop(k, (y + 1 + k) % ys, y).wait_send()
    for j in range(2):
        cross_hop(j).wait_send()
        for d in range(2):
            for u in range(2):
                for s in range(steps_of(j, d)):
                    hop(j, d, u, s).wait_send()


def solution(mesh):
    contexts, heads, xs = mesh.shape["ctx"], mesh.shape["head"], mesh.shape["dp"]
    ys = contexts // 2
    vmem = pl.BlockSpec(memory_space=VMEM)
    smem = pl.BlockSpec(memory_space=pltpu.SMEM)
    dma = pltpu.SemaphoreType.DMA

    def on_device(q, kv, go, act, down, upq, upkv, lengths, order):
        rows, width = q.shape[1], q.shape[2]
        head = kv.shape[3]
        group = width // head
        seq = rows * contexts
        slots = order.shape[0]
        block = seq // slots
        docs = lengths.shape[1]
        rank = upq.shape[0]
        far = ys // 2
        most = ((seq // 2 + block) // TILE + 1) * TILE
        kv = kv.reshape(2, rows, head)
        q, go, act = q.reshape(rows, width), go.reshape(rows, width), act.reshape(rows, width)

        gathered = pl.pallas_call(
            functools.partial(gather_kernel, ys),
            out_shape=jax.ShapeDtypeStruct((2, contexts, rows, head), BF16),
            in_specs=[vmem],
            out_specs=vmem,
            scratch_shapes=[dma((2,)), dma((2, 2, far)), dma((2, 2, far))],
            compiler_params=pltpu.CompilerParams(
                collective_id=0, has_side_effects=True, vmem_limit_bytes=32 << 20
            ),
            name="gather_keys_values",
        )(kv)

        grad_q, parts = pl.pallas_call(
            functools.partial(attention_kernel, group, block, slots, docs),
            out_shape=(
                jax.ShapeDtypeStruct((rows, width), BF16),
                jax.ShapeDtypeStruct((2, seq, head), BF16),
            ),
            in_specs=[smem, smem, vmem, vmem, vmem],
            out_specs=(vmem, vmem),
            scratch_shapes=[
                pltpu.SMEM((slots,), jnp.int32),
                VMEM((TILE + seq, head), BF16),
                VMEM((TILE + seq, head), BF16),
                VMEM((most, group * block), F32),
                VMEM((most, group * block), F32),
                VMEM((2, TILE + seq, head), F32),
            ],
            compiler_params=pltpu.CompilerParams(vmem_limit_bytes=56 << 20),
            name="attention_grads",
        )(order, lengths, q, go, gathered.reshape(2, seq, head))

        width_y = width // ys
        norm = ADAPTER_SCALE / math.sqrt(xs * seq)
        gkv, gdown, gupq, gupkv = pl.pallas_call(
            functools.partial(reduce_kernel, ys, xs, heads, norm),
            out_shape=(
                jax.ShapeDtypeStruct((2, rows, head), BF16),
                jax.ShapeDtypeStruct((3 * rank, width), F32),
                jax.ShapeDtypeStruct((rank, width), F32),
                jax.ShapeDtypeStruct((2, rank, head), F32),
            ),
            in_specs=[vmem] * 6,
            out_specs=(vmem,) * 4,
            scratch_shapes=[
                VMEM((2, 2, 2, far, rows, head), BF16),
                VMEM((2, 2, rows, head), BF16),
                VMEM((heads, 4 * rank, rows), BF16),
                VMEM((heads, 2 * rank, rows), BF16),
                VMEM((ys, 5 * rank, width_y), BF16),
                VMEM((ys, 5 * rank, width_y), BF16),
                VMEM((2 * xs, 5 * rank, width_y), BF16),
                VMEM((ys, 5 * rank, width_y), BF16),
                dma((2, 2, 2, far)),
                dma((2, 2, 2, far)),
                dma((2, 2)),
                dma((heads - 1,)),
                dma((heads - 1,)),
                dma((heads - 1,)),
                dma((heads - 1,)),
                dma((ys - 1,)),
                dma((ys - 1,)),
                dma((2 * xs - 1,)),
                dma((2 * xs - 1,)),
                dma((ys - 1,)),
                dma((ys - 1,)),
            ],
            compiler_params=pltpu.CompilerParams(
                collective_id=1, has_side_effects=True, vmem_limit_bytes=48 << 20
            ),
            name="reduce_grads",
        )(
            parts.reshape(2, contexts, rows, head), grad_q, act,
            down.reshape(3 * rank, width), upq, upkv,
        )
        return (
            grad_q.reshape(1, rows, width),
            gkv.reshape(2, 1, rows, head),
            gdown.reshape(3, rank, width),
            gupq,
            gupkv,
        )

    return jax.shard_map(
        on_device,
        mesh=mesh,
        in_specs=(
            P("dp", "ctx", "head"),
            P(None, "dp", "ctx", "head"),
            P("dp", "ctx", "head"),
            P("dp", "ctx", "head"),
            P(None, None, "head"),
            P(None, "head"),
            P(None, None, "head"),
            P("dp", None),
            P(),
        ),
        out_specs=(
            P("dp", "ctx", "head"),
            P(None, "dp", "ctx", "head"),
            P(None, None, "head"),
            P(None, "head"),
            P(None, None, "head"),
        ),
        check_vma=False,
    )
```

time: 1220 us -> 110 us (0.09)
  the two profiles are of different devices: /device:TPU:64 before, /device:TPU:1 now
where the time goes in v1:
time: 110 us
  Pallas kernels  102 us (93%)
  local copies, waits for them, and re-layouts  6.8 us (6%)
    pallas_call x1, Pallas kernels, on_device(): pl.pallas_call(functools.partial(reduce_kernel, ys, xs, heads, norm), out...  63.9 us
    pallas_call x1, Pallas kernels, on_device(): pl.pallas_call(functools.partial(gather_kernel, ys), out_shape=jax.ShapeD...  30.7 us
    pallas_call x1, Pallas kernels, on_device(): pl.pallas_call(functools.partial(attention_kernel, group, block, slots, d...  7.8 us
    unnamed x20, local copies, waits for them, and re-layouts  6.8 us

profile of v1, /device:TPU:1, one launch (start us, length us, event | category | flops | bytes accessed | tf_op | source)
XLA Modules:
  0.0 109.9 jit_solution(5762109523133611783)
XLA Ops:
  0.6 0.0 copy-start.5
  0.6 0.9 copy-done.5
  1.5 30.7 %gather_keys_values.1 = bf16[2,16,160,128]{3,2,1,0:T(8,128)(2,1)S(1)} custom-call(bf16[2,160,128]{2,1,0:T(8,128)(2,1)S(1)} %bitcast.19), custom_call_target="tpu_custom_call" | custom-call | tf_op jit(solution)/shard_map/gather_keys_values/pallas_call | solution.py:417
  32.3 0.0 copy-start
  32.3 1.1 copy-done
  33.4 0.0 copy-start.2
  33.4 0.0 copy-start.4
  33.4 0.0 copy-start.6
  33.4 0.0 copy-start.7
  33.4 7.8 %attention_grads.1 = (bf16[160,1024]{1,0:T(8,128)(2,1)}, bf16[2,2560,128]{2,1,0:T(8,128)(2,1)}) custom-call(s32[32]{0:T(128)} %order_ref.1, s32[1,8]{1,0:T(1,128)} %lengths_ref.1, bf16[160,1024]{1,0:T(8,128)(2,1)} %bitcast.20, bf16[160,1024]{1,0:T(8,128)(2,1)} %bitcast.21, bf16[2,2560,128]{2,1,0:T(8,128)(2,1)} %bitcast.12), custom_call_target="tpu_custom_call" | custom-call | tf_op jit(solution)/shard_map/attention_grads/pallas_call | solution.py:429
  41.2 0.0 copy-done.2
  41.2 0.0 copy-done.4
  41.2 0.0 copy-done.6
  41.2 0.0 copy-done.7
  41.2 0.0 copy-start.1
  41.2 1.3 %copy-done.1 = bf16[2,2560,128]{2,1,0:T(8,128)(2,1)S(1)} copy-done((bf16[2,2560,128]{2,1,0:T(8,128)(2,1)S(1)}, bf16[2,2560,128]{2,1,0:T(8,128)(2,1)}, u32[]{:S(2)}) %copy-start.1) | copy-done | bytes 1310744
  42.5 0.0 copy-start.3
  42.5 1.0 copy-done.3
  43.5 63.9 %reduce_grads.1 = (bf16[2,160,128]{2,1,0:T(8,128)(2,1)S(1)}, f32[48,1024]{1,0:T(8,128)S(1)}, f32[16,1024]{1,0:T(8,128)S(1)}, f32[2,16,128]{2,1,0:T(8,128)S(1)}) custom-call(bf16[2,16,160,128]{3,2,1,0:T(8,128)(2,1)S(1)} %bitcast.13, bf16[160,1024]{1,0:T(8,128)(2,1)S(1)} %copy-done.3, bf16[160,1024]{1,0:T(8,128)(2,1)S(1)} %bitcast.14, ...), custom_call_target="tpu_custom_call" | custom-call | tf_op jit(solution)/shard_map/reduce_grads/pallas_call | solution.py:451
  107.4 0.6 copy.19
  108.0 0.7 copy.20
  108.7 0.6 copy.21
  109.3 0.6 copy.22
Async XLA Ops:
  0.6 0.9 copy-start.5
  32.3 1.1 copy-start
  33.4 7.8 %copy-start.2 = (bf16[1,160,1024]{2,1,0:T(8,128)(2,1)S(1)}, bf16[1,160,1024]{2,1,0:T(8,128)(2,1)}, u32[]{:S(2)}) copy-start(bf16[1,160,1024]{2,1,0:T(8,128)(2,1)} %param.12) | copy-start | bytes 983044
  33.4 7.8 %copy-start.4 = (bf16[3,16,1024]{2,1,0:T(8,128)(2,1)S(1)}, bf16[3,16,1024]{2,1,0:T(8,128)(2,1)}, u32[]{:S(2)}) copy-start(bf16[3,16,1024]{2,1,0:T(8,128)(2,1)} %param.13) | copy-start | bytes 294916
  33.4 7.8 %copy-start.6 = (bf16[16,1024]{1,0:T(8,128)(2,1)S(1)}, bf16[16,1024]{1,0:T(8,128)(2,1)}, u32[]{:S(2)}) copy-start(bf16[16,1024]{1,0:T(8,128)(2,1)} %upq_ref.1) | copy-start | bytes 98308
  33.4 7.8 %copy-start.7 = (bf16[2,16,128]{2,1,0:T(8,128)(2,1)S(1)}, bf16[2,16,128]{2,1,0:T(8,128)(2,1)}, u32[]{:S(2)}) copy-start(bf16[2,16,128]{2,1,0:T(8,128)(2,1)} %upkv_ref.1) | copy-start | bytes 24580
  41.2 1.3 %copy-start.1 = (bf16[2,2560,128]{2,1,0:T(8,128)(2,1)S(1)}, bf16[2,2560,128]{2,1,0:T(8,128)(2,1)}, u32[]{:S(2)}) copy-start(bf16[2,2560,128]{2,1,0:T(8,128)(2,1)} %get-tuple-element.12) | copy-start | bytes 3932164
  42.5 1.0 copy-start.3

commit v2 on v0

v2 whole, which is shorter than its diff:
```python
import functools
import math

import jax
import jax.numpy as jnp
from jax import lax
from jax.experimental import pallas as pl
from jax.experimental.pallas import tpu as pltpu
from jax.sharding import PartitionSpec as P

MESH = pl.DeviceIdType.MESH
BF16 = jnp.bfloat16
F32 = jnp.float32
VMEM = pltpu.VMEM
NT = (((1,), (1,)), ((), ()))
NN = (((1,), (0,)), ((), ()))
TN = (((0,), (0,)), ((), ()))
ADAPTER_SCALE = 2.0
NEG_LARGE = -1e30
BLOCK_LANES = 256
GATHER_LAG = 3


def dot(a, b, dims):
    return lax.dot_general(a, b, dims, preferred_element_type=F32)


def remote(src, dst, send_sem, recv_sem, device):
    return pltpu.make_async_remote_copy(
        src_ref=src,
        dst_ref=dst,
        send_sem=send_sem,
        recv_sem=recv_sem,
        device_id=device,
        device_id_type=MESH,
    )


def greet(devices):
    barrier = pltpu.get_barrier_semaphore()
    for device in devices:
        pl.semaphore_signal(barrier, inc=1, device_id=device, device_id_type=MESH)
    return barrier


def fused_kernel(
    ys, xs, heads, group, slots_n, docs, norm,
    order_ref, lengths_ref, q_ref, kv_ref, go_ref, act_ref, down_ref, upq_ref, upkv_ref,
    gq_ref, gkv_ref, sum_a, sum_b,
    kv_all, q_st, g_st, s_scr, p_scr, stats, limits, gq_t, own,
    ring_out, ring_in, cross, low_a, low_mine, low_other, low_q, low_kv_out, low_kv,
    ya_out, ya_in, yb_out, yb_in, ga_in, gb_in,
    z_sems, gather_send, gather_recv, ring_send, ring_recv, cross_send, cross_recv,
    la_send, la_recv, lo_sems, lq_send, lq_recv, lk_send, lk_recv, lz_send, lz_recv,
    ya_send, ya_recv, yb_send, yb_recv, ga_send, ga_recv, gb_send, gb_recv,
    aa_send, aa_recv, ab_send, ab_recv,
):
    dp, c, h = lax.axis_index("dp"), lax.axis_index("ctx"), lax.axis_index("head")
    y, z = c % ys, c // ys
    far = ys // 2
    contexts = 2 * ys
    rows, head = kv_ref.shape[1], kv_ref.shape[2]
    rank = upq_ref.shape[0]
    block = rows // 2
    lanes = group * rows
    team = 2 * xs
    factor = 1.0 / math.sqrt(head)
    pieces = lanes // BLOCK_LANES
    tall = rows // 8

    across = (1 - z) * ys + y
    partner = {"ctx": across}
    right = {"ctx": z * ys + (y + 1) % ys}
    left = {"ctx": z * ys + (y + ys - 1) % ys}
    y_peers = [{"ctx": z * ys + (y + k) % ys} for k in range(1, ys)]
    h_peers = [{"head": (h + k) % heads} for k in range(1, heads)]
    z_peers = [{"ctx": across, "head": (h + k) % heads} for k in range(heads)]
    me_t = dp * 2 + z
    t_peers = []
    for k in range(1, team):
        other = (me_t + k) % team
        t_peers.append({"dp": other // 2, "ctx": (other % 2) * ys + y})
    everyone = y_peers + h_peers + z_peers[1:] + t_peers
    barrier = greet(everyone)

    kv_all[:, c] = kv_ref[...]
    act = act_ref[...]
    low_a[h] = dot(down_ref[...], act, NT).astype(BF16)
    for g in range(group):
        q_st[g * rows : (g + 1) * rows] = q_ref[:, g * head : (g + 1) * head]
        g_st[g * rows : (g + 1) * rows] = go_ref[:, g * head : (g + 1) * head]
    lane = lax.broadcasted_iota(jnp.int32, (8, lanes), 1)
    row = lane
    for g in range(1, group):
        row = jnp.where(lane >= g * rows, lane - g * rows, row)
    first = order_ref[2 * c] * block
    second = order_ref[2 * c + 1] * block - block
    pos = row + jnp.where(row < block, first, second)
    begin = jnp.zeros((8, lanes), jnp.int32)
    bound = 0
    for i in range(docs):
        bound = bound + lengths_ref[0, i]
        begin = jnp.where(pos >= bound, bound, begin)
    limits[0] = begin
    limits[1] = pos
    stats[0] = jnp.full((8, lanes), NEG_LARGE, F32)
    stats[1] = jnp.zeros((8, lanes), F32)
    stats[2] = jnp.zeros((8, lanes), F32)
    gq_t[...] = jnp.zeros(gq_t.shape, F32)
    for u in range(2):
        ring_in[0, 1, u, far - 1] = jnp.zeros((rows, head), BF16)
        ring_in[1, 0, u, far - 1] = jnp.zeros((rows, head), BF16)
    pl.semaphore_wait(barrier, len(everyone))

    def spread(buffer, me, peers, size, send, recv):
        def one(k, slot):
            return remote(
                buffer.at[slot], buffer.at[slot], send.at[k], recv.at[k], peers[k]
            )

        def start():
            for k in range(size - 1):
                one(k, me).start()

        def arrive():
            for k in range(size - 1):
                one(k, (me + size - 1 - k) % size).wait_recv()

        def drain():
            for k in range(size - 1):
                one(k, me).wait_send()

        return start, arrive, drain

    def exchange(out, held, send, recv):
        def one(k, to, slot):
            return remote(out.at[to], held.at[slot], send.at[k], recv.at[k], y_peers[k])

        def start():
            for k in range(ys - 1):
                one(k, (y + 1 + k) % ys, y).start()
            held[y] = out[y]

        def arrive():
            for k in range(ys - 1):
                one(k, 0, (y + ys - 1 - k) % ys).wait_recv()

        def drain():
            for k in range(ys - 1):
                one(k, (y + 1 + k) % ys, y).wait_send()

        return start, arrive, drain

    def total_of(buffer, size):
        total = buffer[0].astype(F32)
        for k in range(1, size):
            total = total + buffer[k].astype(F32)
        return total

    cross_kv = remote(
        kv_all.at[:, c], kv_all.at[:, c], z_sems.at[0], z_sems.at[1], partner
    )
    cross_kv.start()

    def line(u):
        return (z + u * (1 - 2 * z)) * ys

    def hop(u, d, s, origin, half):
        slot = line(u) + (origin + ys) % ys
        ref = kv_all.at[d, slot] if half else kv_all.at[:, slot]
        return remote(
            ref, ref, gather_send.at[u, d, s], gather_recv.at[u, d, s],
            right if d == 0 else left,
        )

    def sent(u, d, s, half=False):
        return hop(u, d, s, y - s if d == 0 else y + s, half)

    def landed(u, d, s, half=False):
        return hop(u, d, s, y - 1 - s if d == 0 else y + 1 + s, half)

    for d in range(2):
        sent(0, d, 0).start()
    la_start, la_arrive, la_drain = spread(low_a, h, h_peers, heads, la_send, la_recv)
    la_start()

    sub = lax.broadcasted_iota(jnp.int32, (rows, BLOCK_LANES), 0)
    sub = sub.reshape(tall, 8, BLOCK_LANES)

    def score(slot):
        keys, values = kv_all[0, slot], kv_all[1, slot]
        upper = order_ref[2 * slot] * block
        lower = order_ref[2 * slot + 1] * block - block
        place = sub + jnp.where(sub < block, upper, lower)
        for i in range(pieces):
            at = slice(i * BLOCK_LANES, (i + 1) * BLOCK_LANES)
            s = dot(keys, q_st[at], NT) * (factor * math.log2(math.e))
            s = s.reshape(tall, 8, BLOCK_LANES)
            seen = (place >= limits[0, :, at]) & (place <= limits[1, :, at])
            s = jnp.where(seen, s, NEG_LARGE)
            s_scr[slot, :, at] = s.reshape(rows, BLOCK_LANES)
            d = dot(values, g_st[at], NT)
            p_scr[slot, :, at] = d
            before = stats[0, :, at]
            most = jnp.maximum(before, jnp.max(s, axis=0))
            w = jnp.exp2(s - most)
            shrink = jnp.exp2(before - most)
            stats[0, :, at] = most
            stats[1, :, at] = stats[1, :, at] * shrink + jnp.sum(w, axis=0)
            stats[2, :, at] = stats[2, :, at] * shrink + jnp.sum(
                w * d.reshape(tall, 8, BLOCK_LANES), axis=0
            )

    lag = GATHER_LAG

    def gather_step(k, carry):
        u = k % 2
        n = k // 2 - lag * u

        @pl.when((n >= 0) & (n < ys))
        def _():
            s = (n + 1) // 2
            d = (n + 1) % 2

            @pl.when((u == 1) & (n == 0))
            def _():
                cross_kv.wait_recv()
                for e in range(2):
                    sent(1, e, 0).start()

            @pl.when(((n + 1) % 2 == 0) & (s < far - 1))
            def _():
                for e in range(2):
                    landed(u, e, s - 1).wait_recv()
                    sent(u, e, s).start()

            @pl.when(((n + 1) % 2 == 0) & (s == far - 1))
            def _():
                for e in range(2):
                    landed(u, e, far - 2).wait_recv()
                    sent(u, e, far - 1, True).start()

            @pl.when(n == ys - 1)
            def _():
                for e in range(2):
                    landed(u, e, far - 1, True).wait_recv()

            score(line(u) + (y + 2 * ys + (2 * d - 1) * s) % ys)

        return carry

    lax.fori_loop(0, 2 * ys + 2 * lag, gather_step, 0)

    most = jnp.max(stats[0], axis=0, keepdims=True)
    shrink = jnp.exp2(stats[0] - most)
    total = jnp.sum(stats[1] * shrink, axis=0, keepdims=True)
    slope = jnp.sum(stats[2] * shrink, axis=0, keepdims=True)
    stats[0] = jnp.broadcast_to(most + jnp.log2(total), (8, lanes))
    stats[1] = jnp.broadcast_to(slope / total, (8, lanes))

    def ring(j, d, u, away, to):
        return remote(
            ring_out.at[j, d, u, away - 1], ring_in.at[j, d, u, away - 1],
            ring_send.at[j, d, u, away - 1], ring_recv.at[j, d, u, away - 1], to,
        )

    def reduce_step(k, carry):
        u = k % 2
        n = k // 2
        away = far - (n + 1) // 2
        d = (n + 1) % 2
        slot = line(1 - u) + (y + 2 * ys + (1 - 2 * d) * away) % ys
        keys = kv_all[0, slot]
        grad_k = jnp.zeros((rows, head), F32)
        grad_v = jnp.zeros((rows, head), F32)
        for i in range(pieces):
            at = slice(i * BLOCK_LANES, (i + 1) * BLOCK_LANES)
            s = s_scr[slot, :, at].reshape(tall, 8, BLOCK_LANES)
            prob = jnp.exp2(s - stats[0, :, at])
            tilt = p_scr[slot, :, at].reshape(tall, 8, BLOCK_LANES) - stats[1, :, at]
            ds = (prob * tilt).reshape(rows, BLOCK_LANES).astype(BF16)
            prob = prob.reshape(rows, BLOCK_LANES).astype(BF16)
            grad_v = grad_v + dot(prob, g_st[at], NN)
            grad_k = grad_k + dot(ds, q_st[at], NN)
            gq_t[:, at] += dot(keys, ds, TN)
        grads = (grad_k * factor, grad_v)

        @pl.when(n == 0)
        def _():
            for j in range(2):
                ring_out[j, j, u, far - 1] = grads[j].astype(BF16)
                ring(j, j, u, far, right if j == 0 else left).start()

        for e in range(2):

            @pl.when((n > 0) & (n < ys - 1) & (d == e))
            def _():
                to = right if e == 0 else left
                for j in (1 - e, e):
                    if j == e:
                        ring(j, e, u, away + 1, to).wait_recv()
                    else:

                        @pl.when(away < far - 1)
                        def _():
                            ring(j, e, u, away + 1, to).wait_recv()

                    more = ring_in[j, e, u, away].astype(F32)
                    ring_out[j, e, u, away - 1] = (grads[j] + more).astype(BF16)
                    ring(j, e, u, away, to).start()

        @pl.when(n == ys - 1)
        def _():
            for j in range(2):
                own[u, j] = grads[j]

        return carry

    lax.fori_loop(0, 2 * ys, reduce_step, 0)

    lq_start, lq_arrive, lq_drain = spread(low_q, h, h_peers, heads, lq_send, lq_recv)
    low_x = remote(
        low_mine.at[pl.ds(rank, 2 * rank)], low_other, lo_sems.at[0], lo_sems.at[1], partner
    )
    gq = (gq_t[...] * factor).T.astype(BF16)
    for g in range(group):
        gq_ref[:, g * head : (g + 1) * head] = gq[g * rows : (g + 1) * rows]
    gq = gq_ref[...]
    low_q[h] = dot(upq_ref[...], gq, NT).astype(BF16)
    lq_start()
    la_arrive()
    low = total_of(low_a, heads).astype(BF16)
    low_mine[...] = low
    low_x.start()
    width = act.shape[1] // ys

    def cut(buffer, at, value):
        value = value.astype(BF16)
        for k in range(ys):
            buffer[k, at : at + value.shape[0], :] = value[:, k * width : (k + 1) * width]

    cut(ya_out, rank, dot(low[:rank], gq, NN))

    ends = []
    for u in range(2):
        pair = []
        for j in range(2):
            total = own[u, j]
            for d in range(2):
                ring(j, d, u, 1, right if d == 0 else left).wait_recv()
                total = total + ring_in[j, d, u, 0].astype(F32)
            pair.append(total)
        ends.append(pair)
    cross_hops = [
        remote(cross.at[0, j], cross.at[1, j], cross_send.at[j], cross_recv.at[j], partner)
        for j in range(2)
    ]
    theirs = [ends[0][j].astype(BF16) for j in range(2)]
    ours = [ends[1][j].astype(BF16) for j in range(2)]
    for j in range(2):
        at = slice(j * rank, (j + 1) * rank)
        low_kv[z * heads + h, at, :] = dot(upkv_ref[j], ours[j], NT).astype(BF16)
        low_kv_out[at, :] = dot(upkv_ref[j], theirs[j], NT).astype(BF16)
    me_k = z * heads + h

    def same_hop(k, slot):
        return remote(
            low_kv.at[slot], low_kv.at[slot], lk_send.at[k], lk_recv.at[k], h_peers[k]
        )

    def other_hop(k, slot):
        return remote(low_kv_out, low_kv.at[slot], lz_send.at[k], lz_recv.at[k], z_peers[k])

    for k in range(heads):
        other_hop(k, me_k).start()
    for k in range(heads - 1):
        same_hop(k, me_k).start()
    for j in range(2):
        cross[0, j] = theirs[j]
        own[1, j] = ends[1][j]
        cross_hops[j].start()

    ya_start, ya_arrive, ya_drain = exchange(ya_out, ya_in, ya_send, ya_recv)
    yb_start, yb_arrive, yb_drain = exchange(yb_out, yb_in, yb_send, yb_recv)
    ga_start, ga_arrive, ga_drain = spread(ga_in, me_t, t_peers, team, ga_send, ga_recv)
    gb_start, gb_arrive, gb_drain = spread(gb_in, me_t, t_peers, team, gb_send, gb_recv)
    aa_start, aa_arrive, aa_drain = spread(sum_a, y, y_peers, ys, aa_send, aa_recv)
    ab_start, ab_arrive, ab_drain = spread(sum_b, y, y_peers, ys, ab_send, ab_recv)

    lq_arrive()
    cut(ya_out, 0, dot(total_of(low_q, heads).astype(BF16), act, NN))
    ya_start()
    low_x.wait_recv()
    yb_out[2:, 2 * rank :, :] = jnp.zeros((ys - 2, rank, width), BF16)
    for j in range(2):
        at = slice(j * rank, (j + 1) * rank)
        up = dot(low_mine[(1 + j) * rank : (2 + j) * rank], ours[j], NN)
        up = up + dot(low_other[at], theirs[j], NN)
        yb_out[j, 2 * rank :, :] = up.astype(BF16)
    for k in range(heads):
        other_hop(k, (1 - z) * heads + (h + heads - k) % heads).wait_recv()
    for k in range(heads - 1):
        same_hop(k, z * heads + (h + heads - 1 - k) % heads).wait_recv()
    cut(yb_out, 0, dot(total_of(low_kv, 2 * heads).astype(BF16), act, NN))
    yb_start()
    ya_arrive()
    ga_in[me_t] = total_of(ya_in, ys).astype(BF16)
    ga_start()
    yb_arrive()
    gb_in[me_t] = total_of(yb_in, ys).astype(BF16)
    gb_start()
    ga_arrive()
    sum_a[y] = (total_of(ga_in, team) * norm).astype(BF16)
    aa_start()
    gb_arrive()
    sum_b[y] = (total_of(gb_in, team) * norm).astype(BF16)
    ab_start()
    for j in range(2):
        cross_hops[j].wait_recv()
        gkv_ref[j] = (own[1, j] + cross[1, j].astype(F32)).astype(BF16)
    la_drain()
    lq_drain()
    ya_drain()
    yb_drain()
    ga_drain()
    gb_drain()
    low_x.wait_send()
    cross_kv.wait_send()
    for k in range(heads):
        other_hop(k, me_k).wait_send()
    for k in range(heads - 1):
        same_hop(k, me_k).wait_send()
    for u in range(2):
        for d in range(2):
            for s in range(far):
                sent(u, d, s, s == far - 1).wait_send()
    for j in range(2):
        cross_hops[j].wait_send()
        for d in range(2):
            for u in range(2):
                for away in range(1, far + (j == d)):
                    ring(j, d, u, away, right if d == 0 else left).wait_send()
    aa_arrive()
    ab_arrive()
    aa_drain()
    ab_drain()


def unpack_kernel(
    ys, rank, sum_a, sum_b, gq_in, gkv_in, gq_ref, gkv_ref, gdown_ref, gupq_ref, gupkv_ref
):
    gq_ref[...] = gq_in[...]
    gkv_ref[...] = gkv_in[...]
    width = sum_a.shape[2]
    for k in range(ys):
        at = slice(k * width, (k + 1) * width)
        gdown_ref[:rank, at] = sum_a[k, :rank].astype(F32)
        gupq_ref[:, at] = sum_a[k, rank:].astype(F32)
        gdown_ref[rank:, at] = sum_b[k, : 2 * rank].astype(F32)
    for j in range(2):
        gupkv_ref[j] = sum_b[j, 2 * rank :].astype(F32)


def solution(mesh):
    contexts, heads, xs = mesh.shape["ctx"], mesh.shape["head"], mesh.shape["dp"]
    ys = contexts // 2
    team = 2 * xs
    vmem = pl.BlockSpec(memory_space=VMEM)
    smem = pl.BlockSpec(memory_space=pltpu.SMEM)
    dma = pltpu.SemaphoreType.DMA

    def on_device(q, kv, go, act, down, upq, upkv, lengths, order):
        rows, width = q.shape[1], q.shape[2]
        head = kv.shape[3]
        group = width // head
        lanes = group * rows
        seq = rows * contexts
        slots = order.shape[0]
        docs = lengths.shape[1]
        rank = upq.shape[0]
        far = ys // 2
        kv = kv.reshape(2, rows, head)
        q, go, act = q.reshape(rows, width), go.reshape(rows, width), act.reshape(rows, width)
        wide = width // ys
        norm = ADAPTER_SCALE / math.sqrt(xs * seq)

        grad_q, grad_kv, sum_a, sum_b = pl.pallas_call(
            functools.partial(fused_kernel, ys, xs, heads, group, slots, docs, norm),
            out_shape=(
                jax.ShapeDtypeStruct((rows, width), BF16),
                jax.ShapeDtypeStruct((2, rows, head), BF16),
                jax.ShapeDtypeStruct((ys, 2 * rank, wide), BF16),
                jax.ShapeDtypeStruct((ys, 3 * rank, wide), BF16),
            ),
            in_specs=[smem, smem] + [vmem] * 7,
            out_specs=(vmem,) * 4,
            scratch_shapes=[
                VMEM((2, contexts, rows, head), BF16),
                VMEM((lanes, head), BF16),
                VMEM((lanes, head), BF16),
                VMEM((contexts, rows, lanes), F32),
                VMEM((contexts, rows, lanes), F32),
                VMEM((3, 8, lanes), F32),
                VMEM((2, 8, lanes), jnp.int32),
                VMEM((head, lanes), F32),
                VMEM((2, 2, rows, head), F32),
                VMEM((2, 2, 2, far, rows, head), BF16),
                VMEM((2, 2, 2, far, rows, head), BF16),
                VMEM((2, 2, rows, head), BF16),
                VMEM((heads, 3 * rank, rows), BF16),
                VMEM((3 * rank, rows), BF16),
                VMEM((2 * rank, rows), BF16),
                VMEM((heads, rank, rows), BF16),
                VMEM((2 * rank, rows), BF16),
                VMEM((2 * heads, 2 * rank, rows), BF16),
                VMEM((ys, 2 * rank, wide), BF16),
                VMEM((ys, 2 * rank, wide), BF16),
                VMEM((ys, 3 * rank, wide), BF16),
                VMEM((ys, 3 * rank, wide), BF16),
                VMEM((team, 2 * rank, wide), BF16),
                VMEM((team, 3 * rank, wide), BF16),
                dma((2,)),
                dma((2, 2, far)),
                dma((2, 2, far)),
                dma((2, 2, 2, far)),
                dma((2, 2, 2, far)),
                dma((2,)),
                dma((2,)),
                dma((heads - 1,)),
                dma((heads - 1,)),
                dma((2,)),
                dma((heads - 1,)),
                dma((heads - 1,)),
                dma((heads - 1,)),
                dma((heads - 1,)),
                dma((heads,)),
                dma((heads,)),
            ]
            + [dma((ys - 1,))] * 4
            + [dma((team - 1,))] * 4
            + [dma((ys - 1,))] * 4,
            compiler_params=pltpu.CompilerParams(
                collective_id=0, has_side_effects=True, vmem_limit_bytes=56 << 20
            ),
            name="attention_and_adapter_grads",
        )(order, lengths, q, kv, go, act, down.reshape(3 * rank, width), upq, upkv)

        gq, gkv, gdown, gupq, gupkv = pl.pallas_call(
            functools.partial(unpack_kernel, ys, rank),
            out_shape=(
                jax.ShapeDtypeStruct((rows, width), BF16),
                jax.ShapeDtypeStruct((2, rows, head), BF16),
                jax.ShapeDtypeStruct((3 * rank, width), F32),
                jax.ShapeDtypeStruct((rank, width), F32),
                jax.ShapeDtypeStruct((2, rank, head), F32),
            ),
            in_specs=[vmem] * 4,
            out_specs=(vmem,) * 5,
            name="write_outputs",
        )(sum_a, sum_b, grad_q, grad_kv)
        return (
            gq.reshape(1, rows, width),
            gkv.reshape(2, 1, rows, head),
            gdown.reshape(3, rank, width),
            gupq,
            gupkv,
        )

    return jax.shard_map(
        on_device,
        mesh=mesh,
        in_specs=(
            P("dp", "ctx", "head"),
            P(None, "dp", "ctx", "head"),
            P("dp", "ctx", "head"),
            P("dp", "ctx", "head"),
            P(None, None, "head"),
            P(None, "head"),
            P(None, None, "head"),
            P("dp", None),
            P(),
        ),
        out_specs=(
            P("dp", "ctx", "head"),
            P(None, "dp", "ctx", "head"),
            P(None, None, "head"),
            P(None, "head"),
            P(None, None, "head"),
        ),
        check_vma=False,
    )
```

time: 1220 us -> 87.8 us (0.07)
  the two profiles are of different devices: /device:TPU:64 before, /device:TPU:1 now
where the time goes in v2:
time: 87.8 us; the launch traced here: 86.4 us
  Pallas kernels  85.7 us (98%)
    pallas_call x1, Pallas kernels, on_device(): pl.pallas_call(functools.partial(fused_kernel, ys, xs, heads, group, slot...  83.8 us
    pallas_call x1, Pallas kernels, on_device(): pl.pallas_call(functools.partial(unpack_kernel, ys, rank), out_shape=(jax...  1.91 us

profile of v2, /device:TPU:1, one launch (start us, length us, event | category | flops | bytes accessed | tf_op | source)
XLA Modules:
  0.0 86.4 jit_solution(15867326127120178804)
XLA Ops:
  0.6 83.8 %attention_and_adapter_grads.1 = (bf16[160,1024]{1,0:T(8,128)(2,1)}, bf16[2,160,128]{2,1,0:T(8,128)(2,1)}, bf16[8,32,128]{2,1,0:T(8,128)(2,1)}, bf16[8,48,128]{2,1,0:T(8,128)(2,1)}) custom-call(s32[32]{0:T(128)} %order_ref.1, s32[1,8]{1,0:T(1,128)} %lengths_ref.1, bf16[160,1024]{1,0:T(8,128)(2,1)} %bitcast.10, bf16[2,160,128]{2,1,0:T(8,128)(2,1)} %bitcast.14, ...), custom_call_target="tpu_custom_call" | custom-call | tf_op jit(solution)/shard_map/attention_and_adapter_grads/pallas_call | solution.py:487
  84.5 1.9 %write_outputs.1 = (bf16[160,1024]{1,0:T(8,128)(2,1)}, bf16[2,160,128]{2,1,0:T(8,128)(2,1)}, f32[48,1024]{1,0:T(8,128)}, f32[16,1024]{1,0:T(8,128)}, f32[2,16,128]{2,1,0:T(8,128)}) custom-call(bf16[8,32,128]{2,1,0:T(8,128)(2,1)} %get-tuple-element.14.sum_a, bf16[8,48,128]{2,1,0:T(8,128)(2,1)} %get-tuple-element.15.sum_b, ...), custom_call_target="tpu_custom_call" | custom-call | tf_op jit(solution)/shard_map/write_outputs/pallas_call | solution.py:548

commit v3 on v2

--- a/solution.py
+++ b/solution.py
@@ -18,7 +18,7 @@
 ADAPTER_SCALE = 2.0
 NEG_LARGE = -1e30
 BLOCK_LANES = 256
-GATHER_LAG = 3
+GATHER_LAG = 2
 
 
 def dot(a, b, dims):
@@ -43,15 +43,20 @@
     return barrier
 
 
+def farthest(size):
+    return sorted(range(size - 1), key=lambda k: -min(k + 1, size - 1 - k))
+
+
 def fused_kernel(
     ys, xs, heads, group, slots_n, docs, norm,
     order_ref, lengths_ref, q_ref, kv_ref, go_ref, act_ref, down_ref, upq_ref, upkv_ref,
     gq_ref, gkv_ref, sum_a, sum_b,
-    kv_all, q_st, g_st, s_scr, p_scr, stats, limits, gq_t, own,
-    ring_out, ring_in, cross, low_a, low_mine, low_other, low_q, low_kv_out, low_kv,
-    ya_out, ya_in, yb_out, yb_in, ga_in, gb_in,
-    z_sems, gather_send, gather_recv, ring_send, ring_recv, cross_send, cross_recv,
-    la_send, la_recv, lo_sems, lq_send, lq_recv, lk_send, lk_recv, lz_send, lz_recv,
+    kv_all, q_st, g_st, act_v, s_scr, p_scr, stats, limits, gq_t, own, gq_v,
+    ring_out, ring_in, cross, low_a, low_a2, low_mine, low_other, low_q, low_q2,
+    low_kv, low_kv_out, low_kv2, ya_out, ya_in, yb_out, yb_in, ga_in, gb_in,
+    in_sems, out_sem, z_sems, gather_send, gather_recv, ring_send, ring_recv, cross_send, cross_recv,
+    la_send, la_recv, la2_send, la2_recv, lo_sems, lq_send, lq_recv, lq2_send, lq2_recv,
+    lk_send, lk_recv, lk2_send, lk2_recv, lz_send, lz_recv,
     ya_send, ya_recv, yb_send, yb_recv, ga_send, ga_recv, gb_send, gb_recv,
     aa_send, aa_recv, ab_send, ab_recv,
 ):
@@ -73,22 +78,120 @@
     right = {"ctx": z * ys + (y + 1) % ys}
     left = {"ctx": z * ys + (y + ys - 1) % ys}
     y_peers = [{"ctx": z * ys + (y + k) % ys} for k in range(1, ys)]
-    h_peers = [{"head": (h + k) % heads} for k in range(1, heads)]
-    z_peers = [{"ctx": across, "head": (h + k) % heads} for k in range(heads)]
+    chips = heads // 2
+    core, chip = h % 2, h // 2
+    pair_peers = [{"head": chip * 2 + 1 - core}]
+    chip_heads = [(chip + k) % chips * 2 + core for k in range(chips)]
+    chip_peers = [{"head": other} for other in chip_heads[1:]]
+    z_peers = [{"ctx": across, "head": other} for other in chip_heads]
     me_t = dp * 2 + z
     t_peers = []
     for k in range(1, team):
         other = (me_t + k) % team
         t_peers.append({"dp": other // 2, "ctx": (other % 2) * ys + y})
-    everyone = y_peers + h_peers + z_peers[1:] + t_peers
+    everyone = y_peers + pair_peers + chip_peers + z_peers[1:] + t_peers
     barrier = greet(everyone)
-
-    kv_all[:, c] = kv_ref[...]
-    act = act_ref[...]
-    low_a[h] = dot(down_ref[...], act, NT).astype(BF16)
+    kv_copy = pltpu.make_async_copy(kv_ref, kv_all.at[:, c], in_sems.at[2, 0])
+    act_copy = pltpu.make_async_copy(act_ref, act_v, in_sems.at[2, 1])
+    kv_copy.start()
+    act_copy.start()
+    copies = []
     for g in range(group):
-        q_st[g * rows : (g + 1) * rows] = q_ref[:, g * head : (g + 1) * head]
-        g_st[g * rows : (g + 1) * rows] = go_ref[:, g * head : (g + 1) * head]
+        to = pl.ds(g * rows, rows)
+        of = pl.ds(g * head, head)
+        copies.append(pltpu.make_async_copy(q_ref.at[:, of], q_st.at[to], in_sems.at[0, g]))
+        copies.append(pltpu.make_async_copy(go_ref.at[:, of], g_st.at[to], in_sems.at[1, g]))
+    for copy in copies:
+        copy.start()
+
+    kv_copy.wait()
+    pl.semaphore_wait(barrier, len(everyone))
+
+    def spread(buffer, me, peers, size, send, recv):
+        def one(k, slot):
+            return remote(
+                buffer.at[slot], buffer.at[slot], send.at[k], recv.at[k], peers[k]
+            )
+
+        def start():
+            for k in farthest(size):
+                one(k, me).start()
+
+        def arrive():
+            for k in range(size - 1):
+                one(k, (me + size - 1 - k) % size).wait_recv()
+
+        def drain():
+            for k in range(size - 1):
+                one(k, me).wait_send()
+
+        return start, arrive, drain
+
+    def exchange(out, held, send, recv):
+        def one(k, to, slot):
+            return remote(out.at[to], held.at[slot], send.at[k], recv.at[k], y_peers[k])
+
+        def start():
+            for k in farthest(ys):
+                one(k, (y + 1 + k) % ys, y).start()
+            held[y] = out[y]
+
+        def arrive():
+            for k in range(ys - 1):
+                one(k, 0, (y + ys - 1 - k) % ys).wait_recv()
+
+        def drain():
+            for k in range(ys - 1):
+                one(k, (y + 1 + k) % ys, y).wait_send()
+
+        return start, arrive, drain
+
+    def total_of(buffer, size):
+        total = buffer[0].astype(F32)
+        for k in range(1, size):
+            total = total + buffer[k].astype(F32)
+        return total
+
+    cross_kv = remote(
+        kv_all.at[:, c], kv_all.at[:, c], z_sems.at[0], z_sems.at[1], partner
+    )
+    cross_kv.start()
+
+    def line(u):
+        return (z + u * (1 - 2 * z)) * ys
+
+    def hop(u, d, a, j, here):
+        slot = line(u) + (y + 2 * ys + (2 * d - 1) * here) % ys
+        whole = False
+        ref = kv_all.at[:, slot] if whole else kv_all.at[j, slot]
+        away = 1
+        to = (y + away) % ys if d == 0 else (y + ys - away) % ys
+        return remote(
+            ref, ref, gather_send.at[u, d, a - 1, j], gather_recv.at[u, d, a - 1, j],
+            {"ctx": z * ys + to},
+        )
+
+    def sent(u, d, a, j):
+        return hop(u, d, a, j, a - 1)
+
+    def landed(u, d, a, j):
+        return hop(u, d, a, j, a)
+
+    def messages(u, a):
+        if a == far:
+            return [(d, d) for d in range(2)]
+        return [(d, j) for j in range(2) for d in range(2)]
+
+    for d, j in messages(0, 1):
+        sent(0, d, 1, j).start()
+    la_start, la_arrive, la_drain = spread(low_a, core, pair_peers, 2, la_send, la_recv)
+    la2_start, la2_arrive, la2_drain = spread(
+        low_a2, chip, chip_peers, chips, la2_send, la2_recv
+    )
+    act_copy.wait()
+    act = act_v[...]
+    low_a[core] = dot(down_ref[...], act, NT).astype(BF16)
+    la_start()
     lane = lax.broadcasted_iota(jnp.int32, (8, lanes), 1)
     row = lane
     for g in range(1, group):
@@ -107,83 +210,11 @@
     stats[1] = jnp.zeros((8, lanes), F32)
     stats[2] = jnp.zeros((8, lanes), F32)
     gq_t[...] = jnp.zeros(gq_t.shape, F32)
+    for copy in copies:
+        copy.wait()
     for u in range(2):
         ring_in[0, 1, u, far - 1] = jnp.zeros((rows, head), BF16)
         ring_in[1, 0, u, far - 1] = jnp.zeros((rows, head), BF16)
-    pl.semaphore_wait(barrier, len(everyone))
-
-    def spread(buffer, me, peers, size, send, recv):
-        def one(k, slot):
-            return remote(
-                buffer.at[slot], buffer.at[slot], send.at[k], recv.at[k], peers[k]
-            )
-
-        def start():
-            for k in range(size - 1):
-                one(k, me).start()
-
-        def arrive():
-            for k in range(size - 1):
-                one(k, (me + size - 1 - k) % size).wait_recv()
-
-        def drain():
-            for k in range(size - 1):
-                one(k, me).wait_send()
-
-        return start, arrive, drain
-
-    def exchange(out, held, send, recv):
-        def one(k, to, slot):
-            return remote(out.at[to], held.at[slot], send.at[k], recv.at[k], y_peers[k])
-
-        def start():
-            for k in range(ys - 1):
-                one(k, (y + 1 + k) % ys, y).start()
-            held[y] = out[y]
-
-        def arrive():
-            for k in range(ys - 1):
-                one(k, 0, (y + ys - 1 - k) % ys).wait_recv()
-
-        def drain():
-            for k in range(ys - 1):
-                one(k, (y + 1 + k) % ys, y).wait_send()
-
-        return start, arrive, drain
-
-    def total_of(buffer, size):
-        total = buffer[0].astype(F32)
-        for k in range(1, size):
-            total = total + buffer[k].astype(F32)
-        return total
-
-    cross_kv = remote(
-        kv_all.at[:, c], kv_all.at[:, c], z_sems.at[0], z_sems.at[1], partner
-    )
-    cross_kv.start()
-
-    def line(u):
-        return (z + u * (1 - 2 * z)) * ys
-
-    def hop(u, d, s, origin, half):
-        slot = line(u) + (origin + ys) % ys
-        ref = kv_all.at[d, slot] if half else kv_all.at[:, slot]
-        return remote(
-            ref, ref, gather_send.at[u, d, s], gather_recv.at[u, d, s],
-            right if d == 0 else left,
-        )
-
-    def sent(u, d, s, half=False):
-        return hop(u, d, s, y - s if d == 0 else y + s, half)
-
-    def landed(u, d, s, half=False):
-        return hop(u, d, s, y - 1 - s if d == 0 else y + 1 + s, half)
-
-    for d in range(2):
-        sent(0, d, 0).start()
-    la_start, la_arrive, la_drain = spread(low_a, h, h_peers, heads, la_send, la_recv)
-    la_start()
-
     sub = lax.broadcasted_iota(jnp.int32, (rows, BLOCK_LANES), 0)
     sub = sub.reshape(tall, 8, BLOCK_LANES)
 
@@ -216,36 +247,43 @@
     def gather_step(k, carry):
         u = k % 2
         n = k // 2 - lag * u
+        s = (n + 1) // 2
+        d = (n + 1) % 2
+
+        for a in range(1, far + 1):
+
+            @pl.when(k == 2 * (2 * a - 1))
+            def _():
+                for e, j in messages(0, a):
+                    landed(0, e, a, j).wait_recv()
+                    if a + 1 < far or (a + 1 == far and e == j):
+                        sent(0, e, a + 1, j).start()
+
+        @pl.when(k == 5)
+        def _():
+            cross_kv.wait_recv()
+            for e, j in messages(1, 1):
+                sent(1, e, 1, j).start()
+
+        @pl.when(k == 7)
+        def _():
+            la_arrive()
+            low_a2[chip] = total_of(low_a, 2).astype(BF16)
+            la2_start()
+
+        for a, at in ((1, 1), (2, 3), (3, 5), (4, 7)):
+
+            @pl.when(k == 2 * (at + lag) + 1)
+            def _():
+                for e, j in messages(1, a):
+                    landed(1, e, a, j).wait_recv()
+                    if a + 1 < far or (a + 1 == far and e == j):
+                        sent(1, e, a + 1, j).start()
 
         @pl.when((n >= 0) & (n < ys))
         def _():
-            s = (n + 1) // 2
-            d = (n + 1) % 2
-
-            @pl.when((u == 1) & (n == 0))
-            def _():
-                cross_kv.wait_recv()
-                for e in range(2):
-                    sent(1, e, 0).start()
-
-            @pl.when(((n + 1) % 2 == 0) & (s < far - 1))
-            def _():
-                for e in range(2):
-                    landed(u, e, s - 1).wait_recv()
-                    sent(u, e, s).start()
-
-            @pl.when(((n + 1) % 2 == 0) & (s == far - 1))
-            def _():
-                for e in range(2):
-                    landed(u, e, far - 2).wait_recv()
-                    sent(u, e, far - 1, True).start()
-
-            @pl.when(n == ys - 1)
-            def _():
-                for e in range(2):
-                    landed(u, e, far - 1, True).wait_recv()
-
-            score(line(u) + (y + 2 * ys + (2 * d - 1) * s) % ys)
+            swap = 0
+            score(line(u) + (y + 2 * ys + (2 * d - 1) * (s + swap)) % ys)
 
         return carry
 
@@ -263,6 +301,10 @@
             ring_out.at[j, d, u, away - 1], ring_in.at[j, d, u, away - 1],
             ring_send.at[j, d, u, away - 1], ring_recv.at[j, d, u, away - 1], to,
         )
+
+    low_x = remote(
+        low_mine.at[pl.ds(rank, 2 * rank)], low_other, lo_sems.at[0], lo_sems.at[1], partner
+    )
 
     def reduce_step(k, carry):
         u = k % 2
@@ -285,6 +327,12 @@
             gq_t[:, at] += dot(keys, ds, TN)
         grads = (grad_k * factor, grad_v)
 
+        @pl.when(k == 3)
+        def _():
+            la2_arrive()
+            low_mine[...] = total_of(low_a2, chips).astype(BF16)
+            low_x.start()
+
         @pl.when(n == 0)
         def _():
             for j in range(2):
@@ -318,20 +366,20 @@
 
     lax.fori_loop(0, 2 * ys, reduce_step, 0)
 
-    lq_start, lq_arrive, lq_drain = spread(low_q, h, h_peers, heads, lq_send, lq_recv)
-    low_x = remote(
-        low_mine.at[pl.ds(rank, 2 * rank)], low_other, lo_sems.at[0], lo_sems.at[1], partner
+    lq_start, lq_arrive, lq_drain = spread(low_q, core, pair_peers, 2, lq_send, lq_recv)
+    lq2_start, lq2_arrive, lq2_drain = spread(
+        low_q2, chip, chip_peers, chips, lq2_send, lq2_recv
     )
+    lk_start, lk_arrive, lk_drain = spread(low_kv, core, pair_peers, 2, lk_send, lk_recv)
     gq = (gq_t[...] * factor).T.astype(BF16)
     for g in range(group):
-        gq_ref[:, g * head : (g + 1) * head] = gq[g * rows : (g + 1) * rows]
-    gq = gq_ref[...]
-    low_q[h] = dot(upq_ref[...], gq, NT).astype(BF16)
+        gq_v[:, g * head : (g + 1) * head] = gq[g * rows : (g + 1) * rows]
+    gq_copy = pltpu.make_async_copy(gq_v, gq_ref, out_sem)
+    gq_copy.start()
+    gq = gq_v[...]
+    low_q[core] = dot(upq_ref[...], gq, NT).astype(BF16)
     lq_start()
-    la_arrive()
-    low = total_of(low_a, heads).astype(BF16)
-    low_mine[...] = low
-    low_x.start()
+    low = low_mine[...]
     width = act.shape[1] // ys
 
     def cut(buffer, at, value):
@@ -340,6 +388,10 @@
             buffer[k, at : at + value.shape[0], :] = value[:, k * width : (k + 1) * width]
 
     cut(ya_out, rank, dot(low[:rank], gq, NN))
+
+    lq_arrive()
+    low_q2[chip] = total_of(low_q, 2).astype(BF16)
+    lq2_start()
 
     ends = []
     for u in range(2):
@@ -359,26 +411,36 @@
     ours = [ends[1][j].astype(BF16) for j in range(2)]
     for j in range(2):
         at = slice(j * rank, (j + 1) * rank)
-        low_kv[z * heads + h, at, :] = dot(upkv_ref[j], ours[j], NT).astype(BF16)
-        low_kv_out[at, :] = dot(upkv_ref[j], theirs[j], NT).astype(BF16)
-    me_k = z * heads + h
+        low_kv[core, 0, at, :] = dot(upkv_ref[j], ours[j], NT).astype(BF16)
+        low_kv[core, 1, at, :] = dot(upkv_ref[j], theirs[j], NT).astype(BF16)
+    lk_start()
+    me_k = z * chips + chip
 
     def same_hop(k, slot):
         return remote(
-            low_kv.at[slot], low_kv.at[slot], lk_send.at[k], lk_recv.at[k], h_peers[k]
+            low_kv2.at[slot], low_kv2.at[slot], lk2_send.at[k], lk2_recv.at[k], chip_peers[k]
         )
 
     def other_hop(k, slot):
-        return remote(low_kv_out, low_kv.at[slot], lz_send.at[k], lz_recv.at[k], z_peers[k])
-
-    for k in range(heads):
-        other_hop(k, me_k).start()
-    for k in range(heads - 1):
-        same_hop(k, me_k).start()
+        return remote(low_kv_out, low_kv2.at[slot], lz_send.at[k], lz_recv.at[k], z_peers[k])
+
     for j in range(2):
         cross[0, j] = theirs[j]
         own[1, j] = ends[1][j]
-        cross_hops[j].start()
+    low_x.wait_recv()
+    ya_out[2:, 2 * rank :, :] = jnp.zeros((ys - 2, rank, width), BF16)
+    for j in range(2):
+        at = slice(j * rank, (j + 1) * rank)
+        up = dot(low_mine[(1 + j) * rank : (2 + j) * rank], ours[j], NN)
+        up = up + dot(low_other[at], theirs[j], NN)
+        ya_out[j, 2 * rank :, :] = up.astype(BF16)
+    lk_arrive()
+    low_kv2[me_k] = (low_kv[0, 0].astype(F32) + low_kv[1, 0].astype(F32)).astype(BF16)
+    low_kv_out[...] = (low_kv[0, 1].astype(F32) + low_kv[1, 1].astype(F32)).astype(BF16)
+    for k in range(chips):
+        other_hop(k, me_k).start()
+    for k in range(chips - 1):
+        same_hop(k, me_k).start()
 
     ya_start, ya_arrive, ya_drain = exchange(ya_out, ya_in, ya_send, ya_recv)
     yb_start, yb_arrive, yb_drain = exchange(yb_out, yb_in, yb_send, yb_recv)
@@ -387,21 +449,14 @@
     aa_start, aa_arrive, aa_drain = spread(sum_a, y, y_peers, ys, aa_send, aa_recv)
     ab_start, ab_arrive, ab_drain = spread(sum_b, y, y_peers, ys, ab_send, ab_recv)
 
-    lq_arrive()
-    cut(ya_out, 0, dot(total_of(low_q, heads).astype(BF16), act, NN))
+    lq2_arrive()
+    cut(ya_out, 0, dot(total_of(low_q2, chips).astype(BF16), act, NN))
     ya_start()
-    low_x.wait_recv()
-    yb_out[2:, 2 * rank :, :] = jnp.zeros((ys - 2, rank, width), BF16)
-    for j in range(2):
-        at = slice(j * rank, (j + 1) * rank)
-        up = dot(low_mine[(1 + j) * rank : (2 + j) * rank], ours[j], NN)
-        up = up + dot(low_other[at], theirs[j], NN)
-        yb_out[j, 2 * rank :, :] = up.astype(BF16)
-    for k in range(heads):
-        other_hop(k, (1 - z) * heads + (h + heads - k) % heads).wait_recv()
-    for k in range(heads - 1):
-        same_hop(k, z * heads + (h + heads - 1 - k) % heads).wait_recv()
-    cut(yb_out, 0, dot(total_of(low_kv, 2 * heads).astype(BF16), act, NN))
+    for k in range(chips):
+        other_hop(k, (1 - z) * chips + (chip + chips - k) % chips).wait_recv()
+    for k in range(chips - 1):
+        same_hop(k, z * chips + (chip + chips - 1 - k) % chips).wait_recv()
+    cut(yb_out, 0, dot(total_of(low_kv2, 2 * chips).astype(BF16), act, NN))
     yb_start()
     ya_arrive()
     ga_in[me_t] = total_of(ya_in, ys).astype(BF16)
@@ -416,24 +471,29 @@
     sum_b[y] = (total_of(gb_in, team) * norm).astype(BF16)
     ab_start()
     for j in range(2):
+        cross_hops[j].start()
+    for j in range(2):
         cross_hops[j].wait_recv()
         gkv_ref[j] = (own[1, j] + cross[1, j].astype(F32)).astype(BF16)
     la_drain()
+    la2_drain()
     lq_drain()
+    lq2_drain()
+    lk_drain()
     ya_drain()
     yb_drain()
     ga_drain()
     gb_drain()
     low_x.wait_send()
     cross_kv.wait_send()
-    for k in range(heads):
+    for k in range(chips):
         other_hop(k, me_k).wait_send()
-    for k in range(heads - 1):
+    for k in range(chips - 1):
         same_hop(k, me_k).wait_send()
     for u in range(2):
-        for d in range(2):
-            for s in range(far):
-                sent(u, d, s, s == far - 1).wait_send()
+        for a in range(1, far + 1):
+            for d, j in messages(u, a):
+                sent(u, d, a, j).wait_send()
     for j in range(2):
         cross_hops[j].wait_send()
         for d in range(2):
@@ -444,6 +504,7 @@
     ab_arrive()
     aa_drain()
     ab_drain()
+    gq_copy.wait()
 
 
 def unpack_kernel(
@@ -455,18 +516,19 @@
     for k in range(ys):
         at = slice(k * width, (k + 1) * width)
         gdown_ref[:rank, at] = sum_a[k, :rank].astype(F32)
-        gupq_ref[:, at] = sum_a[k, rank:].astype(F32)
-        gdown_ref[rank:, at] = sum_b[k, : 2 * rank].astype(F32)
+        gupq_ref[:, at] = sum_a[k, rank : 2 * rank].astype(F32)
+        gdown_ref[rank:, at] = sum_b[k].astype(F32)
     for j in range(2):
-        gupkv_ref[j] = sum_b[j, 2 * rank :].astype(F32)
+        gupkv_ref[j] = sum_a[j, 2 * rank :].astype(F32)
 
 
 def solution(mesh):
     contexts, heads, xs = mesh.shape["ctx"], mesh.shape["head"], mesh.shape["dp"]
     ys = contexts // 2
-    team = 2 * xs
+    team, chips = 2 * xs, heads // 2
     vmem = pl.BlockSpec(memory_space=VMEM)
     smem = pl.BlockSpec(memory_space=pltpu.SMEM)
+    anywhere = pl.BlockSpec(memory_space=pl.ANY)
     dma = pltpu.SemaphoreType.DMA
 
     def on_device(q, kv, go, act, down, upq, upkv, lengths, order):
@@ -489,52 +551,65 @@
             out_shape=(
                 jax.ShapeDtypeStruct((rows, width), BF16),
                 jax.ShapeDtypeStruct((2, rows, head), BF16),
+                jax.ShapeDtypeStruct((ys, 3 * rank, wide), BF16),
                 jax.ShapeDtypeStruct((ys, 2 * rank, wide), BF16),
-                jax.ShapeDtypeStruct((ys, 3 * rank, wide), BF16),
             ),
-            in_specs=[smem, smem] + [vmem] * 7,
-            out_specs=(vmem,) * 4,
+            in_specs=[smem, smem] + [anywhere] * 4 + [vmem] * 3,
+            out_specs=(anywhere, vmem, vmem, vmem),
             scratch_shapes=[
                 VMEM((2, contexts, rows, head), BF16),
                 VMEM((lanes, head), BF16),
                 VMEM((lanes, head), BF16),
+                VMEM((rows, width), BF16),
                 VMEM((contexts, rows, lanes), F32),
                 VMEM((contexts, rows, lanes), F32),
                 VMEM((3, 8, lanes), F32),
                 VMEM((2, 8, lanes), jnp.int32),
                 VMEM((head, lanes), F32),
                 VMEM((2, 2, rows, head), F32),
+                VMEM((rows, width), BF16),
                 VMEM((2, 2, 2, far, rows, head), BF16),
                 VMEM((2, 2, 2, far, rows, head), BF16),
                 VMEM((2, 2, rows, head), BF16),
-                VMEM((heads, 3 * rank, rows), BF16),
+                VMEM((2, 3 * rank, rows), BF16),
+                VMEM((chips, 3 * rank, rows), BF16),
                 VMEM((3 * rank, rows), BF16),
                 VMEM((2 * rank, rows), BF16),
-                VMEM((heads, rank, rows), BF16),
+                VMEM((2, rank, rows), BF16),
+                VMEM((chips, rank, rows), BF16),
+                VMEM((2, 2, 2 * rank, rows), BF16),
                 VMEM((2 * rank, rows), BF16),
-                VMEM((2 * heads, 2 * rank, rows), BF16),
+                VMEM((2 * chips, 2 * rank, rows), BF16),
+                VMEM((ys, 3 * rank, wide), BF16),
+                VMEM((ys, 3 * rank, wide), BF16),
                 VMEM((ys, 2 * rank, wide), BF16),
                 VMEM((ys, 2 * rank, wide), BF16),
-                VMEM((ys, 3 * rank, wide), BF16),
-                VMEM((ys, 3 * rank, wide), BF16),
+                VMEM((team, 3 * rank, wide), BF16),
                 VMEM((team, 2 * rank, wide), BF16),
-                VMEM((team, 3 * rank, wide), BF16),
+                dma((3, group)),
+                dma,
                 dma((2,)),
-                dma((2, 2, far)),
-                dma((2, 2, far)),
+                dma((2, 2, far, 2)),
+                dma((2, 2, far, 2)),
                 dma((2, 2, 2, far)),
                 dma((2, 2, 2, far)),
                 dma((2,)),
                 dma((2,)),
-                dma((heads - 1,)),
-                dma((heads - 1,)),
+                dma((1,)),
+                dma((1,)),
+                dma((chips - 1,)),
+                dma((chips - 1,)),
                 dma((2,)),
-                dma((heads - 1,)),
-                dma((heads - 1,)),
-                dma((heads - 1,)),
-                dma((heads - 1,)),
-                dma((heads,)),
-                dma((heads,)),
+                dma((1,)),
+                dma((1,)),
+                dma((chips - 1,)),
+                dma((chips - 1,)),
+                dma((1,)),
+                dma((1,)),
+                dma((chips - 1,)),
+                dma((chips - 1,)),
+                dma((chips,)),
+                dma((chips,)),
             ]
             + [dma((ys - 1,))] * 4
             + [dma((team - 1,))] * 4

time: 87.8 us -> 84.4 us (0.961)
  Pallas kernels: 85.7 us -> 82.8 us
    pallas_call x1, Pallas kernels: 83.8 us -> 80.9 us  [on_device(): pl.pallas_call(functools.partial(fused_kernel, ys, xs, heads, group, slot...]
where the time goes in v3:
time: 84.4 us; the launch traced here: 83.4 us
  Pallas kernels  82.8 us (98%)
    pallas_call x1, Pallas kernels, on_device(): pl.pallas_call(functools.partial(fused_kernel, ys, xs, heads, group, slot...  80.9 us
    pallas_call x1, Pallas kernels, on_device(): pl.pallas_call(functools.partial(unpack_kernel, ys, rank), out_shape=(jax...  1.92 us

profile of v3, /device:TPU:1, one launch (start us, length us, event | category | flops | bytes accessed | tf_op | source)
XLA Modules:
  0.0 83.4 jit_solution(2304306701136566122)
XLA Ops:
  0.6 80.9 %attention_and_adapter_grads.1 = (bf16[160,1024]{1,0:T(8,128)(2,1)}, bf16[2,160,128]{2,1,0:T(8,128)(2,1)}, bf16[8,48,128]{2,1,0:T(8,128)(2,1)}, bf16[8,32,128]{2,1,0:T(8,128)(2,1)}) custom-call(s32[32]{0:T(128)} %order_ref.1, s32[1,8]{1,0:T(1,128)} %lengths_ref.1, bf16[160,1024]{1,0:T(8,128)(2,1)} %bitcast.10, bf16[2,160,128]{2,1,0:T(8,128)(2,1)} %bitcast.14, ...), custom_call_target="tpu_custom_call" | custom-call | tf_op jit(solution)/shard_map/attention_and_adapter_grads/pallas_call | solution.py:549
  81.5 1.9 %write_outputs.1 = (bf16[160,1024]{1,0:T(8,128)(2,1)}, bf16[2,160,128]{2,1,0:T(8,128)(2,1)}, f32[48,1024]{1,0:T(8,128)}, f32[16,1024]{1,0:T(8,128)}, f32[2,16,128]{2,1,0:T(8,128)}) custom-call(bf16[8,48,128]{2,1,0:T(8,128)(2,1)} %get-tuple-element.14.sum_a, bf16[8,32,128]{2,1,0:T(8,128)(2,1)} %get-tuple-element.15.sum_b, ...), custom_call_target="tpu_custom_call" | custom-call | tf_op jit(solution)/shard_map/write_outputs/pallas_call | solution.py:623

commit v4 on v3

--- a/solution.py
+++ b/solution.py
@@ -89,7 +89,7 @@
     for k in range(1, team):
         other = (me_t + k) % team
         t_peers.append({"dp": other // 2, "ctx": (other % 2) * ys + y})
-    everyone = y_peers + pair_peers + chip_peers + z_peers[1:] + t_peers
+    everyone = t_peers + z_peers[1:] + y_peers + chip_peers + pair_peers
     barrier = greet(everyone)
     kv_copy = pltpu.make_async_copy(kv_ref, kv_all.at[:, c], in_sems.at[2, 0])
     act_copy = pltpu.make_async_copy(act_ref, act_v, in_sems.at[2, 1])
@@ -164,7 +164,7 @@
         slot = line(u) + (y + 2 * ys + (2 * d - 1) * here) % ys
         whole = False
         ref = kv_all.at[:, slot] if whole else kv_all.at[j, slot]
-        away = 1
+        away = 2 if u == 1 and a == far else 1
         to = (y + away) % ys if d == 0 else (y + ys - away) % ys
         return remote(
             ref, ref, gather_send.at[u, d, a - 1, j], gather_recv.at[u, d, a - 1, j],
@@ -172,7 +172,7 @@
         )
 
     def sent(u, d, a, j):
-        return hop(u, d, a, j, a - 1)
+        return hop(u, d, a, j, a - 2 if u == 1 and a == far else a - 1)
 
     def landed(u, d, a, j):
         return hop(u, d, a, j, a)
@@ -212,9 +212,6 @@
     gq_t[...] = jnp.zeros(gq_t.shape, F32)
     for copy in copies:
         copy.wait()
-    for u in range(2):
-        ring_in[0, 1, u, far - 1] = jnp.zeros((rows, head), BF16)
-        ring_in[1, 0, u, far - 1] = jnp.zeros((rows, head), BF16)
     sub = lax.broadcasted_iota(jnp.int32, (rows, BLOCK_LANES), 0)
     sub = sub.reshape(tall, 8, BLOCK_LANES)
 
@@ -277,7 +274,9 @@
             def _():
                 for e, j in messages(1, a):
                     landed(1, e, a, j).wait_recv()
-                    if a + 1 < far or (a + 1 == far and e == j):
+                    if a == far - 2 and e == j:
+                        sent(1, e, far, j).start()
+                    if a + 1 < far:
                         sent(1, e, a + 1, j).start()
 
         @pl.when((n >= 0) & (n < ys))
@@ -305,6 +304,8 @@
     low_x = remote(
         low_mine.at[pl.ds(rank, 2 * rank)], low_other, lo_sems.at[0], lo_sems.at[1], partner
     )
+
+    skip = [{"ctx": z * ys + (y + 2) % ys}, {"ctx": z * ys + (y + ys - 2) % ys}]
 
     def reduce_step(k, carry):
         u = k % 2
@@ -337,25 +338,24 @@
         def _():
             for j in range(2):
                 ring_out[j, j, u, far - 1] = grads[j].astype(BF16)
-                ring(j, j, u, far, right if j == 0 else left).start()
+                ring(j, j, u, far, skip[j]).start()
 
         for e in range(2):
-
-            @pl.when((n > 0) & (n < ys - 1) & (d == e))
-            def _():
-                to = right if e == 0 else left
-                for j in (1 - e, e):
-                    if j == e:
-                        ring(j, e, u, away + 1, to).wait_recv()
-                    else:
-
-                        @pl.when(away < far - 1)
-                        def _():
-                            ring(j, e, u, away + 1, to).wait_recv()
-
-                    more = ring_in[j, e, u, away].astype(F32)
-                    ring_out[j, e, u, away - 1] = (grads[j] + more).astype(BF16)
-                    ring(j, e, u, away, to).start()
+            to = right if e == 0 else left
+            for a in range(far - 1, 0, -1):
+
+                @pl.when((n > 0) & (n < ys - 1) & (d == e) & (away == a))
+                def _():
+                    for j in (1 - e, e):
+                        part = grads[j]
+                        if a < far - 1:
+                            ring(j, e, u, a + 1, to).wait_recv()
+                            part = part + ring_in[j, e, u, a].astype(F32)
+                        if a == far - 2 and j == e:
+                            ring(j, e, u, far, to).wait_recv()
+                            part = part + ring_in[j, e, u, far - 1].astype(F32)
+                        ring_out[j, e, u, a - 1] = part.astype(BF16)
+                        ring(j, e, u, a, to).start()
 
         @pl.when(n == ys - 1)
         def _():
@@ -468,10 +468,10 @@
     sum_a[y] = (total_of(ga_in, team) * norm).astype(BF16)
     aa_start()
     gb_arrive()
+    for j in range(2):
+        cross_hops[j].start()
     sum_b[y] = (total_of(gb_in, team) * norm).astype(BF16)
     ab_start()
-    for j in range(2):
-        cross_hops[j].start()
     for j in range(2):
         cross_hops[j].wait_recv()
         gkv_ref[j] = (own[1, j] + cross[1, j].astype(F32)).astype(BF16)

time: 84.4 us -> 84.2 us (level)
  no operation moved by 1% of the time
where the time goes in v4:
time: 84.2 us; the launch traced here: 83.3 us
  Pallas kernels  82.6 us (98%)
    pallas_call x1, Pallas kernels, on_device(): pl.pallas_call(functools.partial(fused_kernel, ys, xs, heads, group, slot...  80.7 us
    pallas_call x1, Pallas kernels, on_device(): pl.pallas_call(functools.partial(unpack_kernel, ys, rank), out_shape=(jax...  1.92 us

profile of v4, /device:TPU:1, one launch (start us, length us, event | category | flops | bytes accessed | tf_op | source)
XLA Modules:
  0.0 83.3 jit_solution(15752256773992994440)
XLA Ops:
  0.6 80.7 %attention_and_adapter_grads.1 = (bf16[160,1024]{1,0:T(8,128)(2,1)}, bf16[2,160,128]{2,1,0:T(8,128)(2,1)}, bf16[8,48,128]{2,1,0:T(8,128)(2,1)}, bf16[8,32,128]{2,1,0:T(8,128)(2,1)}) custom-call(s32[32]{0:T(128)} %order_ref.1, s32[1,8]{1,0:T(1,128)} %lengths_ref.1, bf16[160,1024]{1,0:T(8,128)(2,1)} %bitcast.10, bf16[2,160,128]{2,1,0:T(8,128)(2,1)} %bitcast.14, ...), custom_call_target="tpu_custom_call" | custom-call | tf_op jit(solution)/shard_map/attention_and_adapter_grads/pallas_call | solution.py:549
  81.3 1.9 %write_outputs.1 = (bf16[160,1024]{1,0:T(8,128)(2,1)}, bf16[2,160,128]{2,1,0:T(8,128)(2,1)}, f32[48,1024]{1,0:T(8,128)}, f32[16,1024]{1,0:T(8,128)}, f32[2,16,128]{2,1,0:T(8,128)}) custom-call(bf16[8,48,128]{2,1,0:T(8,128)(2,1)} %get-tuple-element.14.sum_a, bf16[8,32,128]{2,1,0:T(8,128)(2,1)} %get-tuple-element.15.sum_b, ...), custom_call_target="tpu_custom_call" | custom-call | tf_op jit(solution)/shard_map/write_outputs/pallas_call | solution.py:623
